TPU v7x, 128 devices: a whole 4x4x4 slice. The times are simulated.
128 devices in a mesh: row: 8 (over z, y_hi), col: 8 (over x, y_lo), dp: 2 (over core).
Axes of the slice: x: 4, y: 4 (y_hi: 2, y_lo: 2; y = y_hi * 2 + y_lo), z: 4, core: 2. Of those that a mesh axis runs over, the one named last changes fastest.
Arguments:
- tokens: bfloat16 [2048, 6144], P(('dp', 'col'), 'row'), may hold values from -6 to 6
- up_weight: bfloat16 [6144, 24576], P('row', 'col'), may hold values from -0.078125 to 0.078125
- down_weight: bfloat16 [24576, 6144], P('col', 'row'), may hold values from -0.0390625 to 0.0390625
- cotangent: bfloat16 [2048, 6144], P(('dp', 'col'), 'row'), may hold values from -6 to 6
Outputs:
- mlp_output: bfloat16 [2048, 6144], P(('dp', 'col'), 'row')
- input_grad: bfloat16 [2048, 6144], P(('dp', 'col'), 'row')
- up_grad: float32 [6144, 24576], P('row', ('col', 'dp'))
- down_grad: float32 [24576, 6144], P(('col', 'dp'), 'row')
All inputs are finite; a program needn't handle non-finite values.
Results may differ from a plain program's by a relative error of at most 0.03.
Values may be sent and summed in bfloat16 or wider, within the bound.
A program may use at most 192 MiB of HBM per device.

v0:
```python
import jax
import jax.numpy as jnp
from jax import lax
from jax.sharding import PartitionSpec as P

ROOT_HALF = 0.7071067811865476
DENSITY = 0.3989422804014327


def gelu_exact(values):
    return 0.5 * values * (1.0 + lax.erf(values * ROOT_HALF))


def gelu_slope(values):
    return 0.5 * (1.0 + lax.erf(values * ROOT_HALF)) + values * DENSITY * jnp.exp(
        -0.5 * values * values
    )


def contract_last(matrix_a, matrix_b):
    return lax.dot_general(
        matrix_a, matrix_b, (((1,), (1,)), ((), ())), preferred_element_type=jnp.float32
    )


def contract_first(matrix_a, matrix_b):
    return lax.dot_general(
        matrix_a, matrix_b, (((0,), (0,)), ((), ())), preferred_element_type=jnp.float32
    )


def on_device(tokens, up_weight, down_weight, cotangent):
    gathered, incoming = (
        lax.all_gather(tokens, "col", axis=0, tiled=True),
        lax.all_gather(cotangent, "col", axis=0, tiled=True),
    )
    partial_up = jnp.dot(gathered, up_weight, preferred_element_type=jnp.float32)
    partial_back = contract_last(incoming, down_weight)
    preact, back_sum = (
        lax.psum(partial_up.astype(jnp.bfloat16), "row").astype(jnp.float32),
        lax.psum(partial_back.astype(jnp.bfloat16), "row").astype(jnp.float32),
    )
    activated = gelu_exact(preact).astype(jnp.bfloat16)
    hidden_grad = (back_sum * gelu_slope(preact)).astype(jnp.bfloat16)
    mlp_output = lax.psum_scatter(
        jnp.dot(activated, down_weight, preferred_element_type=jnp.float32).astype(jnp.bfloat16),
        "col",
        scatter_dimension=0,
        tiled=True,
    )
    input_grad = lax.psum_scatter(
        contract_last(hidden_grad, up_weight).astype(jnp.bfloat16),
        "col",
        scatter_dimension=0,
        tiled=True,
    )
    up_grad = lax.psum_scatter(
        contract_first(gathered, hidden_grad).astype(jnp.bfloat16),
        "dp",
        scatter_dimension=1,
        tiled=True,
    ).astype(jnp.float32)
    down_grad = lax.psum_scatter(
        contract_first(activated, incoming).astype(jnp.bfloat16),
        "dp",
        scatter_dimension=0,
        tiled=True,
    ).astype(jnp.float32)
    return (mlp_output, input_grad, up_grad, down_grad)


def solution(mesh):
    placed = (P(("dp", "col"), "row"), P("row", "col"), P("col", "row"), P(("dp", "col"), "row"))
    return jax.shard_map(
        on_device,
        mesh=mesh,
        in_specs=placed,
        out_specs=(
            P(("dp", "col"), "row"),
            P(("dp", "col"), "row"),
            P("row", ("col", "dp")),
            P(("col", "dp"), "row"),
        ),
        check_vma=False,
    )
```

profile of v0, /device:TPU:0, one launch (start us, length us, event | category | flops | bytes accessed | tf_op | source)
XLA Modules:
  0.0 772.6 jit_solution(8541156320167344694)
XLA Ops:
  7.2 0.0 all-gather.5.cloned.1.call-start
  7.2 0.7 all-gather.5.cloned.1.call-update
  7.9 0.0 all-gather.3.cloned.1.call-start
  7.9 0.7 all-gather.3.cloned.1.call-update
  8.6 0.0 all-reduce.3.cloned.1.call-start
  8.7 46.9 %all-gather.5.cloned.1.call-done = bf16[1024,768]{1,0:T(8,128)(2,1)} async-done(((bf16[128,768]{1,0:T(8,128)(2,1)}), bf16[1024,768]{1,0:T(8,128)(2,1)}) %all-gather.5.cloned.1.call-update) | async-done | bytes 1572880 | tf_op jit(solution)/shard_map/all_gather | solution.py:35
  55.5 9.2 %convolution_convert_fusion = bf16[1024,3072]{1,0:T(8,128)(2,1)} fusion(bf16[1024,768]{1,0:T(8,128)(2,1)} %all-gather.5.cloned.1.call-done, bf16[3072,768]{1,0:T(8,128)(2,1)} %param.6), kind=kOutput, calls=%fused_computation.14 | convolution fusion | flops 4834983936 | bytes 12582912 | tf_op jit(solution)/shard_map/dot_general | solution.py:21
  64.7 36.1 %all-gather.3.cloned.1.call-done = bf16[1024,768]{1,0:T(8,128)(2,1)} async-done(((bf16[128,768]{1,0:T(8,128)(2,1)}), bf16[1024,768]{1,0:T(8,128)(2,1)}) %all-gather.3.cloned.1.call-update) | async-done | bytes 1572880 | tf_op jit(solution)/shard_map/all_gather | solution.py:34
  100.8 9.0 %convolution_convert_fusion.1 = bf16[1024,3072]{1,0:T(8,128)(2,1)} fusion(bf16[1024,768]{1,0:T(8,128)(2,1)} %all-gather.3.cloned.1.call-done, bf16[768,3072]{1,0:T(8,128)(2,1)} %param.5), kind=kOutput, calls=%fused_computation.15 | convolution fusion | flops 4834983936 | bytes 12582912 | tf_op jit(solution)/shard_map/dot_general | solution.py:37
  109.8 0.0 all-reduce.3.cloned.1.call-update
  109.9 0.0 reduce-scatter.11.cloned.1.call-start
  109.9 500.3 %all-reduce.3.cloned.1.call-done = (bf16[1024,3072]{1,0:T(8,128)(2,1)}, bf16[1024,3072]{1,0:T(8,128)(2,1)}) async-done(((bf16[1024,3072]{1,0:T(8,128)(2,1)}, bf16[1024,3072]{1,0:T(8,128)(2,1)}), (bf16[1024,3072]{1,0:T(8,128)(2,1)}, bf16[1024,3072]{1,0:T(8,128)(2,1)})) %all-reduce.3.cloned.1.call-update) | async-done | bytes 12582928 | tf_op jit(solution)/shard_map/psum | solution.py:40
  610.2 0.0 copy-start.1
  610.2 0.0 copy-start.3
  610.2 12.6 %fusion.7 = (bf16[1024,3072]{1,0:T(8,128)(2,1)}, f32[1024,3072]{1,0:T(8,128)S(1)}) fusion(bf16[1024,3072]{1,0:T(8,128)(2,1)} %get-tuple-element.8, bf16[1024,3072]{1,0:T(8,128)(2,1)} %get-tuple-element.9), kind=kLoop, calls=%fused_computation.12 | loop fusion | flops 37748736 | bytes 31457280 | tf_op jit(solution)/shard_map/convert_element_type | solution.py:44
  622.8 0.0 copy-start
  622.8 4.5 copy-done
  627.3 0.0 copy-done.1
  627.3 0.0 copy-done.3
  627.3 0.0 copy-start.2
  627.3 7.6 convolution_convert_fusion.2
  634.9 0.0 reduce-scatter.11.cloned.1.call-update
  634.9 0.0 reduce-scatter.9.cloned.1.call-start
  635.0 0.0 copy-done.2
  635.0 9.7 %fusion.9 = bf16[768,3072]{0,1:T(8,128)(2,1)} fusion(bf16[1024,3072]{1,0:T(8,128)(2,1)} %get-tuple-element.10, bf16[1024,768]{1,0:T(8,128)(2,1)S(1)} %copy-done.2), kind=kOutput, calls=%fused_computation.18 | convolution fusion | flops 4834197504 | bytes 12582912 | tf_op jit(solution)/shard_map/dot_general | solution.py:27
  644.6 0.0 reduce-scatter.9.cloned.1.call-update
  644.7 0.0 reduce-scatter.7.cloned.1.call-start
  644.7 10.7 %convolution_convert_fusion.4 = bf16[1024,768]{1,0:T(8,128)(2,1)} fusion(bf16[1024,3072]{1,0:T(8,128)(2,1)} %get-tuple-element.10, bf16[768,3072]{1,0:T(8,128)(2,1)} %param.5), kind=kOutput, calls=%fused_computation.19 | convolution fusion | flops 4832624640 | bytes 12582912 | tf_op jit(solution)/shard_map/dot_general | solution.py:21
  655.5 0.0 reduce-scatter.7.cloned.1.call-update
  655.5 0.2 reduce-scatter.5.cloned.1.call-start
  655.7 11.3 %convolution_convert_fusion.5 = bf16[1024,768]{1,0:T(8,128)(2,1)} fusion(bf16[3072,768]{1,0:T(8,128)(2,1)} %param.6, f32[1024,3072]{1,0:T(8,128)} %copy-done, bf16[1024,3072]{1,0:T(8,128)(2,1)} %get-tuple-element.8), kind=kOutput, calls=%fused_computation.20 | convolution fusion | flops 4845207552 | bytes 25165824 | tf_op jit(solution)/shard_map/dot_general | solution.py:46
  667.0 0.0 reduce-scatter.5.cloned.1.call-update
  667.0 0.0 reduce-scatter.11.cloned.1.call-done
  667.0 4.5 convert_element_type.51
  671.5 0.0 reduce-scatter.9.cloned.1.call-done
  671.5 4.6 copy.8
  676.1 42.9 %reduce-scatter.7.cloned.1.call-done = bf16[128,768]{1,0:T(8,128)(2,1)} async-done(((bf16[1024,768]{1,0:T(8,128)(2,1)}), bf16[128,768]{1,0:T(8,128)(2,1)}) %reduce-scatter.7.cloned.1.call-update) | async-done | bytes 196624 | tf_op jit(solution)/shard_map/reduce_scatter | solution.py:51
  718.9 46.8 %reduce-scatter.5.cloned.1.call-done = bf16[128,768]{1,0:T(8,128)(2,1)} async-done(((bf16[1024,768]{1,0:T(8,128)(2,1)}), bf16[128,768]{1,0:T(8,128)(2,1)}) %reduce-scatter.5.cloned.1.call-update) | async-done | bytes 196624 | tf_op jit(solution)/shard_map/reduce_scatter | solution.py:45
Async XLA Ops:
  7.2 48.4 %all-gather.5.cloned.1.call-start = ((), (), s32[]{:S(2)}) async-start(), calls=%async_computation.6 | async-start | bytes 1769472 | tf_op jit(solution)/shard_map/all_gather | solution.py:35
  7.9 92.9 %all-gather.3.cloned.1.call-start = ((), (), s32[]{:S(2)}) async-start(), calls=%async_computation.4 | async-start | bytes 1769472 | tf_op jit(solution)/shard_map/all_gather | solution.py:34
  8.6 601.5 %all-reduce.3.cloned.1.call-start = ((), (), s32[]{:S(2)}) async-start(), calls=%async_computation.10 | async-start | bytes 25165824 | tf_op jit(solution)/shard_map/psum | solution.py:40
  109.9 557.2 %reduce-scatter.11.cloned.1.call-start = ((), (), s32[]{:S(2)}) async-start(), calls=%async_computation.9 | async-start | bytes 7077888 | tf_op jit(solution)/shard_map/reduce_scatter | solution.py:63
  610.2 17.1 %copy-start.1 = (bf16[1024,3072]{1,0:T(8,128)(2,1)S(1)}, bf16[1024,3072]{1,0:T(8,128)(2,1)}, u32[]{:S(2)}) copy-start(bf16[1024,3072]{1,0:T(8,128)(2,1)} %get-tuple-element.8) | copy-start | bytes 18874372
  610.2 17.1 %copy-start.3 = (bf16[1024,768]{1,0:T(8,128)(2,1)S(1)}, bf16[1024,768]{1,0:T(8,128)(2,1)}, u32[]{:S(2)}) copy-start(bf16[1024,768]{1,0:T(8,128)(2,1)} %all-gather.5.cloned.1.call-done) | copy-start | bytes 4718596
  622.8 4.5 copy-start
  627.3 7.6 copy-start.2
  634.9 36.6 %reduce-scatter.9.cloned.1.call-start = ((), (), s32[]{:S(2)}) async-start(), calls=%async_computation.8 | async-start | bytes 7077888 | tf_op jit(solution)/shard_map/reduce_scatter | solution.py:57
  644.7 74.3 %reduce-scatter.7.cloned.1.call-start = ((), (), s32[]{:S(2)}) async-start(), calls=%async_computation.7 | async-start | bytes 1769472 | tf_op jit(solution)/shard_map/reduce_scatter | solution.py:51
  655.5 110.3 %reduce-scatter.5.cloned.1.call-start = ((), (), s32[]{:S(2)}) async-start(), calls=%async_computation.5 | async-start | bytes 1769472 | tf_op jit(solution)/shard_map/reduce_scatter | solution.py:45
Sparse Core Ops, SparseCore 0:
  9.6 45.8 all-gather.4
  57.2 43.5 all-gather.2
  110.0 500.1 all-reduce.2
  635.0 15.3 reduce-scatter.10
  653.4 16.6 reduce-scatter.8
  672.9 45.9 reduce-scatter.6
  721.9 43.8 reduce-scatter.4
where the time goes:
time: 773 us
  waiting for transfers between devices  674 us (87%)
  matrix products  57.4 us (7%)
  other arithmetic  17.1 us (2%)
  between operations  14.1 us (2%)
  local copies, waits for them, and re-layouts  9.08 us (1%)
    psum x1, waiting for transfers between devices, on_device(): lax.psum(partial_up.astype(jnp.bfloat16), 'row').astype(jnp.float32)  500 us
    all_gather x1, waiting for transfers between devices, on_device(): lax.all_gather(cotangent, 'col', axis=0, tiled=True)  46.9 us
    reduce_scatter x1, waiting for transfers between devices, on_device(): lax.psum_scatter(jnp.dot(activated, down_weight, preferred_element_type=j...  46.8 us
    reduce_scatter x1, waiting for transfers between devices, on_device(): lax.psum_scatter(contract_last(hidden_grad, up_weight).astype(jnp.bfloat1...  42.9 us
    all_gather x1, waiting for transfers between devices, on_device(): lax.all_gather(tokens, 'col', axis=0, tiled=True)  36.1 us
    dot_general x2, matrix products, contract_last(): lax.dot_general(matrix_a, matrix_b, (((1,), (1,)), ((), ())), preferred_e...  19.9 us
    dot_general x2, matrix products, contract_first(): lax.dot_general(matrix_a, matrix_b, (((0,), (0,)), ((), ())), preferred_e...  17.2 us
  transfers between devices with their start and end apart: 7, of which 5 were waited for; matrix products, arithmetic and copies ran while one was open for 6% of the time, Pallas kernels for 0%

commit v1 on v0

v1 whole, which is shorter than its diff:
```python
import jax
import jax.numpy as jnp
from jax import lax
from jax.sharding import Mesh, PartitionSpec as P

ROOT_HALF = 0.7071067811865476
DENSITY = 0.3989422804014327


def contract_last(matrix_a, matrix_b):
    return lax.dot_general(
        matrix_a, matrix_b, (((1,), (1,)), ((), ())), preferred_element_type=jnp.float32
    )


def contract_first(matrix_a, matrix_b):
    return lax.dot_general(
        matrix_a, matrix_b, (((0,), (0,)), ((), ())), preferred_element_type=jnp.float32
    )


def on_device(tokens, up_weight, down_weight, cotangent):
    yh = lax.axis_index("yh")
    half = up_weight.shape[1] // 2
    gathered, incoming = (
        lax.all_gather(lax.all_gather(part, "yh", axis=1, tiled=True), ("x", "yl"), axis=0, tiled=True)
        for part in (tokens, cotangent)
    )
    swap = [(0, 1), (1, 0)]
    up_mine = lax.dynamic_slice_in_dim(up_weight, yh * half, half, 1)
    up_theirs = lax.ppermute(lax.dynamic_slice_in_dim(up_weight, (1 - yh) * half, half, 1), "yh", swap)
    down_mine = lax.dynamic_slice_in_dim(down_weight, yh * half, half, 0)
    down_theirs = lax.ppermute(
        lax.dynamic_slice_in_dim(down_weight, (1 - yh) * half, half, 0), "yh", swap
    )
    up = jnp.where(
        yh == 0,
        jnp.concatenate([up_mine, up_theirs], 0),
        jnp.concatenate([up_theirs, up_mine], 0),
    )
    down = jnp.where(
        yh == 0,
        jnp.concatenate([down_mine, down_theirs], 1),
        jnp.concatenate([down_theirs, down_mine], 1),
    )
    bf = jnp.bfloat16
    partial_up = jnp.dot(gathered, up, preferred_element_type=jnp.float32).astype(bf)
    partial_back = contract_last(incoming, down).astype(bf)
    preact = lax.psum_scatter(partial_up, "z", scatter_dimension=0, tiled=True).astype(jnp.float32)
    back_sum = lax.psum_scatter(partial_back, "z", scatter_dimension=0, tiled=True).astype(jnp.float32)
    cdf = 0.5 * (1.0 + lax.erf(preact * ROOT_HALF))
    activated = (preact * cdf).astype(bf)
    hidden_grad = (back_sum * (cdf + preact * DENSITY * jnp.exp(-0.5 * preact * preact))).astype(bf)
    activated = lax.all_gather(activated, "z", axis=0, tiled=True)
    hidden_grad = lax.all_gather(hidden_grad, "z", axis=0, tiled=True)

    def spread(part):
        part = lax.psum_scatter(part.astype(bf), "yh", scatter_dimension=1, tiled=True)
        return lax.psum_scatter(part, ("x", "yl"), scatter_dimension=0, tiled=True)

    mlp_output = spread(jnp.dot(activated, down, preferred_element_type=jnp.float32))
    input_grad = spread(contract_last(hidden_grad, up))
    across = [(0, 0), (1, 2), (2, 1), (3, 3)]
    up_grad = lax.psum_scatter(
        contract_first(gathered, hidden_grad).astype(bf), "dp", scatter_dimension=0, tiled=True
    )
    up_grad = lax.ppermute(up_grad, ("yh", "dp"), across)
    down_grad = lax.psum_scatter(
        contract_first(activated, incoming).astype(bf), "dp", scatter_dimension=1, tiled=True
    )
    down_grad = lax.ppermute(down_grad, ("yh", "dp"), across)
    return (mlp_output, input_grad, up_grad.astype(jnp.float32), down_grad.astype(jnp.float32))


def solution(mesh):
    fine = Mesh(mesh.devices.reshape(4, 2, 4, 2, 2), ("z", "yh", "x", "yl", "dp"))
    rows = P(("dp", "x", "yl"), ("z", "yh"))
    return jax.shard_map(
        on_device,
        mesh=fine,
        in_specs=(rows, P(("z", "yh"), ("x", "yl")), P(("x", "yl"), ("z", "yh")), rows),
        out_specs=(rows, rows, P(("z", "yh"), ("x", "yl", "dp")), P(("x", "yl", "dp"), ("z", "yh"))),
        check_vma=False,
    )
```

time: 773 us -> 639 us (0.83)
  waiting for transfers between devices: 674 us -> 498 us
  starting transfers between devices: 0.46 us -> 24.9 us
  blocking collectives: 0 us -> 19.3 us
  other arithmetic: 17.1 us -> 5.87 us
    psum x1 -> x0, waiting for transfers between devices: 500 us -> none  [on_device(): lax.psum(partial_up.astype(jnp.bfloat16), 'row').astype(jnp.float32)]
    ppermute x0 -> x4, waiting for transfers between devices: none -> 203 us  [the longest x1 125 us: on_device(): lax.ppermute(lax.dynamic_slice_in_dim(up_weight, (1 - yh) * half, half, 1...]
    reduce_scatter x4 -> x8, waiting for transfers between devices: 89.7 us -> 216 us  [the longest x2 74.3 us: spread(): return lax.psum_scatter(part, ('x', 'yl'), scatter_dimension=0, tiled=True)]
    ppermute x0 -> x4, starting transfers between devices: none -> 24.1 us  [the longest x1 19.3 us: on_device(): up_grad = lax.ppermute(up_grad, ('yh', 'dp'), across)]
    all_gather x0 -> x2, blocking collectives: none -> 19.3 us  [on_device(): lax.all_gather(part, 'yh', axis=1, tiled=True)]
    convert_element_type x2, other arithmetic: 17.1 us -> 5.87 us  [the longest x1 3.32 us: on_device(): (back_sum * (cdf + preact * DENSITY * jnp.exp(-0.5 * preact * preact))).a...]
    dynamic_slice x0 -> x2, local copies, waits for them, and re-layouts: none -> 8.34 us  [the longest x1 4.22 us: on_device(): up_mine = lax.dynamic_slice_in_dim(up_weight, yh * half, half, 1)]
    all_gather x2 -> x4, waiting for transfers between devices: 82.9 us -> 78.6 us  [the longest x1 42.3 us: on_device(): hidden_grad = lax.all_gather(hidden_grad, 'z', axis=0, tiled=True)]
  transfers between devices with their start and end apart: 7 -> 16, of which waited for: 5 -> 11; matrix products, arithmetic and copies ran while one was open for 6% -> 11% of each run, Pallas kernels for 0% -> 0%
where the time goes in v1:
time: 639 us; the launch traced here: 637 us
  waiting for transfers between devices  498 us (78%)
  matrix products  57.3 us (9%)
  starting transfers between devices  24.9 us (4%)
  blocking collectives  19.3 us (3%)
  local copies, waits for them, and re-layouts  16.5 us (3%)
  between operations  14.2 us (2%)
    ppermute x1, waiting for transfers between devices, on_device(): lax.ppermute(lax.dynamic_slice_in_dim(up_weight, (1 - yh) * half, half, 1...  125 us
    ppermute x1, waiting for transfers between devices, on_device(): lax.ppermute(lax.dynamic_slice_in_dim(down_weight, (1 - yh) * half, half,...  78.3 us
    reduce_scatter x2, waiting for transfers between devices, spread(): return lax.psum_scatter(part, ('x', 'yl'), scatter_dimension=0, tiled=True)  74.3 us
    reduce_scatter x2, waiting for transfers between devices, spread(): lax.psum_scatter(part.astype(bf), 'yh', scatter_dimension=1, tiled=True)  68.2 us
    all_gather x1, waiting for transfers between devices, on_device(): hidden_grad = lax.all_gather(hidden_grad, 'z', axis=0, tiled=True)  42.3 us
    reduce_scatter x1, waiting for transfers between devices, on_device(): lax.psum_scatter(partial_back, 'z', scatter_dimension=0, tiled=True)  38.1 us
    all_gather x1, waiting for transfers between devices, on_device(): activated = lax.all_gather(activated, 'z', axis=0, tiled=True)  36.3 us
    dot_general x2, matrix products, contract_last(): lax.dot_general(matrix_a, matrix_b, (((1,), (1,)), ((), ())), preferred_e...  20.5 us
  transfers between devices with their start and end apart: 16, of which 11 were waited for; matrix products, arithmetic and copies ran while one was open for 11% of the time, Pallas kernels for 0%

profile of v1, /device:TPU:0, one launch (start us, length us, event | category | flops | bytes accessed | tf_op | source)
XLA Modules:
  0.0 636.5 jit_solution(9111242810337972732)
XLA Ops:
  7.2 0.0 all-gather.5.cloned.1.call-start
  7.2 10.8 %all_gather.18 = bf16[128,1536]{1,0:T(8,128)(2,1)} all-gather(bf16[128,768]{1,0:T(8,128)(2,1)} %param.4), channel_id=1, replica_groups=mesh['z'=4,'yh'=2,'x'=4,'yl'=2,'dp'=2] {'yh'}, dimensions={1}, use_global_device_ids=true | all-gather | bytes 589824 | tf_op jit(solution)/shard_map/all_gather | solution.py:26
  18.0 0.0 all-gather.5.cloned.1.call-update
  18.0 0.0 all-gather.9.cloned.1.call-start
  18.0 8.6 %all_gather.21 = bf16[128,1536]{1,0:T(8,128)(2,1)} all-gather(bf16[128,768]{1,0:T(8,128)(2,1)} %param.7), channel_id=1, replica_groups=mesh['z'=4,'yh'=2,'x'=4,'yl'=2,'dp'=2] {'yh'}, dimensions={1}, use_global_device_ids=true | all-gather | bytes 589824 | tf_op jit(solution)/shard_map/all_gather | solution.py:26
  26.6 0.0 all-gather.9.cloned.1.call-update
  26.6 0.0 reduce-scatter.9.cloned.1.call-start
  26.7 4.2 constant_dynamic-slice_fusion.3
  30.9 1.8 collective-permute-start
  32.7 125.1 %collective-permute-done = bf16[768,1536]{1,0:T(8,128)(2,1)} collective-permute-done((bf16[768,1536]{1,0:T(8,128)(2,1)}, bf16[768,1536]{1,0:T(8,128)(2,1)}, u32[]{:S(2)}, u32[]{:S(2)}) %collective-permute-start) | collective-permute-done | bytes 2359328 | tf_op jit(solution)/shard_map/ppermute | solution.py:31
  157.8 9.1 %fusion.1 = bf16[1024,1536]{0,1:T(8,128)(2,1)} fusion(bf16[1024,1536]{1,0:T(8,128)(2,1)} %all-gather.5.cloned.1.call-done, bf16[768,1536]{1,0:T(8,128)(2,1)} %collective-permute-done, bf16[768,1536]{1,0:T(8,128)(2,1)S(1)} %get-tuple-element.10, pred[]{:T(512)S(6)} %eq.4), kind=kOutput, calls=%fused_computation.9 | convolution fusion | flops 4854644736 | bytes 11010049 | tf_op jit(solution)/shard_map/dot_general | solution.py:47
  167.0 0.0 reduce-scatter.9.cloned.1.call-update
  167.0 0.0 reduce-scatter.15.cloned.1.call-start
  167.0 4.1 constant_dynamic-slice_fusion.1
  171.2 0.7 collective-permute-start.1
  171.9 78.3 %collective-permute-done.1 = bf16[1536,768]{1,0:T(8,128)(2,1)} collective-permute-done((bf16[1536,768]{1,0:T(8,128)(2,1)S(1)}, bf16[1536,768]{1,0:T(8,128)(2,1)}, u32[]{:S(2)}, u32[]{:S(2)}) %collective-permute-start.1) | collective-permute-done | bytes 2359328 | tf_op jit(solution)/shard_map/ppermute | solution.py:33
  250.2 10.5 %fusion.2 = bf16[1024,1536]{0,1:T(8,128)(2,1)} fusion(bf16[1024,1536]{1,0:T(8,128)(2,1)} %all-gather.9.cloned.1.call-done, bf16[1536,768]{1,0:T(8,128)(2,1)} %collective-permute-done.1, bf16[1536,768]{1,0:T(8,128)(2,1)} %get-tuple-element.8, pred[]{:T(512)S(6)} %eq.4), kind=kOutput, calls=%fused_computation.10 | convolution fusion | flops 4854644736 | bytes 11010049 | tf_op jit(solution)/shard_map/dot_general | solution.py:11
  260.7 0.0 all-gather.11.cloned.1.call-start
  260.7 0.0 reduce-scatter.9.cloned.1.call-done
  260.8 38.1 %reduce-scatter.15.cloned.1.call-done = bf16[256,1536]{0,1:T(8,128)(2,1)} async-done(((bf16[1024,1536]{0,1:T(8,128)(2,1)}), bf16[256,1536]{0,1:T(8,128)(2,1)}) %reduce-scatter.15.cloned.1.call-update) | async-done | bytes 786448 | tf_op jit(solution)/shard_map/reduce_scatter | solution.py:50
  298.9 3.3 fusion.10
  302.2 0.0 all-gather.11.cloned.1.call-update
  302.2 0.0 all-gather.7.cloned.1.call-start
  302.3 0.5 all-gather.7.cloned.1.call-update
  302.8 0.2 reduce-scatter.17.cloned.1.call-start
  303.0 42.3 %all-gather.11.cloned.1.call-done = bf16[1024,1536]{0,1:T(8,128)(2,1)} async-done(((bf16[256,1536]{0,1:T(8,128)(2,1)}), bf16[1024,1536]{0,1:T(8,128)(2,1)}) %all-gather.11.cloned.1.call-update) | async-done | bytes 3145744 | tf_op jit(solution)/shard_map/all_gather | solution.py:55
  345.4 10.0 %convolution_convert_fusion.2 = bf16[1024,1536]{1,0:T(8,128)(2,1)} fusion(bf16[1024,1536]{0,1:T(8,128)(2,1)} %all-gather.11.cloned.1.call-done, bf16[768,1536]{1,0:T(8,128)(2,1)} %collective-permute-done, bf16[768,1536]{1,0:T(8,128)(2,1)S(1)} %get-tuple-element.10, pred[]{:T(512)S(6)} %eq.4), kind=kOutput, calls=%fused_computation.5 | convolution fusion | flops 4854644736 | bytes 11010049 | tf_op jit(solution)/shard_map/dot_general | solution.py:11
  355.4 0.0 reduce-scatter.11.cloned.1.call-start
  355.5 36.3 %all-gather.7.cloned.1.call-done = bf16[1024,1536]{0,1:T(8,128)(2,1)} async-done(((bf16[256,1536]{0,1:T(8,128)(2,1)}), bf16[1024,1536]{0,1:T(8,128)(2,1)}) %all-gather.7.cloned.1.call-update) | async-done | bytes 3145744 | tf_op jit(solution)/shard_map/all_gather | solution.py:54
  391.7 10.1 %convolution_convert_fusion.4 = bf16[1024,1536]{1,0:T(8,128)(2,1)} fusion(bf16[1024,1536]{0,1:T(8,128)(2,1)} %all-gather.7.cloned.1.call-done, bf16[1536,768]{1,0:T(8,128)(2,1)} %collective-permute-done.1, bf16[1536,768]{1,0:T(8,128)(2,1)S(1)} %copy-done, pred[]{:T(512)S(6)} %eq.4), kind=kOutput, calls=%fused_computation.7 | convolution fusion | flops 4854644736 | bytes 11010049 | tf_op jit(solution)/shard_map/dot_general | solution.py:61
  401.9 0.3 reduce-scatter.23.cloned.1.call-start
  402.1 1.7 copy-done.2
  403.9 9.0 %convolution_convert_fusion = bf16[1536,1536]{1,0:T(8,128)(2,1)} fusion(bf16[1024,1536]{0,1:T(8,128)(2,1)} %all-gather.7.cloned.1.call-done, bf16[1024,1536]{1,0:T(8,128)(2,1)S(1)} %copy-done.2), kind=kOutput, calls=%fused_computation | convolution fusion | flops 4834197504 | bytes 11010048 | tf_op jit(solution)/shard_map/dot_general | solution.py:17
  412.9 0.0 reduce-scatter.21.cloned.1.call-start
  412.9 1.8 copy-done.1
  414.7 8.6 %fusion = bf16[1536,1536]{0,1:T(8,128)(2,1)} fusion(bf16[1024,1536]{0,1:T(8,128)(2,1)} %all-gather.11.cloned.1.call-done, bf16[1024,1536]{1,0:T(8,128)(2,1)S(1)} %copy-done.1), kind=kOutput, calls=%fused_computation.2 | convolution fusion | flops 4834197504 | bytes 11010048 | tf_op jit(solution)/shard_map/dot_general | solution.py:17
  423.3 0.0 reduce-scatter.19.cloned.1.call-start
  423.4 19.0 %reduce-scatter.17.cloned.1.call-done = bf16[1024,768]{1,0:T(8,128)(2,1)} async-done(((bf16[1024,1536]{1,0:T(8,128)(2,1)}), bf16[1024,768]{1,0:T(8,128)(2,1)}) %reduce-scatter.17.cloned.1.call-update) | async-done | bytes 1572880 | tf_op jit(solution)/shard_map/reduce_scatter | solution.py:58
  442.4 0.0 reduce-scatter.13.cloned.1.call-start
  442.4 49.2 %reduce-scatter.11.cloned.1.call-done = bf16[1024,768]{1,0:T(8,128)(2,1)} async-done(((bf16[1024,1536]{1,0:T(8,128)(2,1)}), bf16[1024,768]{1,0:T(8,128)(2,1)}) %reduce-scatter.11.cloned.1.call-update) | async-done | bytes 1572880 | tf_op jit(solution)/shard_map/reduce_scatter | solution.py:58
  491.7 17.6 %reduce-scatter.23.cloned.1.call-done = bf16[1536,768]{1,0:T(8,128)(2,1)} async-done(((bf16[1536,1536]{1,0:T(8,128)(2,1)}), bf16[1536,768]{1,0:T(8,128)(2,1)}) %reduce-scatter.23.cloned.1.call-update) | async-done | bytes 2359312 | tf_op jit(solution)/shard_map/reduce_scatter | solution.py:68
  509.3 2.3 collective-permute-start.3
  511.6 17.3 %reduce-scatter.21.cloned.1.call-done = bf16[768,1536]{0,1:T(8,128)(2,1)} async-done(((bf16[1536,1536]{0,1:T(8,128)(2,1)}), bf16[768,1536]{0,1:T(8,128)(2,1)}) %reduce-scatter.21.cloned.1.call-update) | async-done | bytes 2359312 | tf_op jit(solution)/shard_map/reduce_scatter | solution.py:64
  528.9 19.3 %collective-permute-start.2 = (bf16[768,1536]{0,1:T(8,128)(2,1)}, bf16[768,1536]{0,1:T(8,128)(2,1)}, u32[]{:S(2)}, u32[]{:S(2)}) collective-permute-start(bf16[768,1536]{0,1:T(8,128)(2,1)} %reduce-scatter.21.cloned.1.call-done), channel_id=1, source_target_pairs={{0,0},{1,16},{16,1},{17,17},{2,2},{3,18},{18,3},{19,19},{4,4},{5,2... | collective-permute-start | bytes 7077896 | tf_op jit(solution)/shard_map/ppermute | solution.py:67
  548.2 2.5 convert_element_type.59
  550.8 4.6 copy.8
  555.3 26.8 %reduce-scatter.19.cloned.1.call-done = bf16[128,768]{1,0:T(8,128)(2,1)} async-done(((bf16[1024,768]{1,0:T(8,128)(2,1)}), bf16[128,768]{1,0:T(8,128)(2,1)}) %reduce-scatter.19.cloned.1.call-update) | async-done | bytes 196624 | tf_op jit(solution)/shard_map/reduce_scatter | solution.py:59
  582.1 47.5 %reduce-scatter.13.cloned.1.call-done = bf16[128,768]{1,0:T(8,128)(2,1)} async-done(((bf16[1024,768]{1,0:T(8,128)(2,1)}), bf16[128,768]{1,0:T(8,128)(2,1)}) %reduce-scatter.13.cloned.1.call-update) | async-done | bytes 196624 | tf_op jit(solution)/shard_map/reduce_scatter | solution.py:59
  (15 shorter events, 0.1 us)
Async XLA Ops:
  7.2 150.7 %all-gather.5.cloned.1.call-start = ((), (), s32[]{:S(2)}) async-start(), calls=%async_computation.8 | async-start | bytes 3538944 | tf_op jit(solution)/shard_map/all_gather | solution.py:26
  18.0 232.2 %all-gather.9.cloned.1.call-start = ((), (), s32[]{:S(2)}) async-start(), calls=%async_computation.13 | async-start | bytes 3538944 | tf_op jit(solution)/shard_map/all_gather | solution.py:26
  26.6 234.1 %reduce-scatter.9.cloned.1.call-start = ((), (), s32[]{:S(2)}) async-start(), calls=%async_computation.9 | async-start | bytes 3932160 | tf_op jit(solution)/shard_map/reduce_scatter | solution.py:49
  30.9 126.9 %collective-permute-start = (bf16[768,1536]{1,0:T(8,128)(2,1)}, bf16[768,1536]{1,0:T(8,128)(2,1)}, u32[]{:S(2)}, u32[]{:S(2)}) collective-permute-start(bf16[768,1536]{1,0:T(8,128)(2,1)} %get-tuple-element.11), channel_id=1, source_target_pairs={{0,16},{16,0},{1,17},{17,1},{2,18},{18,2},{3,19},{19,3},{4,20},{20... | collective-permute-start | bytes 7077896 | tf_op jit(solution)/shard_map/ppermute | solution.py:31
  167.0 131.9 %reduce-scatter.15.cloned.1.call-start = ((), (), s32[]{:S(2)}) async-start(), calls=%async_computation.14 | async-start | bytes 3932160 | tf_op jit(solution)/shard_map/reduce_scatter | solution.py:50
  171.2 79.0 %collective-permute-start.1 = (bf16[1536,768]{1,0:T(8,128)(2,1)S(1)}, bf16[1536,768]{1,0:T(8,128)(2,1)}, u32[]{:S(2)}, u32[]{:S(2)}) collective-permute-start(bf16[1536,768]{1,0:T(8,128)(2,1)S(1)} %get-tuple-element.9), channel_id=1, source_target_pairs={{0,16},{16,0},{1,17},{17,1},{2,18},{18,2},{3,19},{19,3},{4,20},{20... | collective-permute-start | bytes 7077896 | tf_op jit(solution)/shard_map/ppermute | solution.py:33
  260.7 84.7 %all-gather.11.cloned.1.call-start = ((), (), s32[]{:S(2)}) async-start(), calls=%async_computation.15 | async-start | bytes 3932160 | tf_op jit(solution)/shard_map/all_gather | solution.py:55
  302.2 89.5 %all-gather.7.cloned.1.call-start = ((), (), s32[]{:S(2)}) async-start(), calls=%async_computation.10 | async-start | bytes 3932160 | tf_op jit(solution)/shard_map/all_gather | solution.py:54
  302.8 139.5 %reduce-scatter.17.cloned.1.call-start = ((), (), s32[]{:S(2)}) async-start(), calls=%async_computation.16 | async-start | bytes 4718592 | tf_op jit(solution)/shard_map/reduce_scatter | solution.py:58
  355.4 36.3 %copy-start = (bf16[1536,768]{1,0:T(8,128)(2,1)S(1)}, bf16[1536,768]{1,0:T(8,128)(2,1)}, u32[]{:S(2)}) copy-start(bf16[1536,768]{1,0:T(8,128)(2,1)} %get-tuple-element.8) | copy-start | bytes 7077892
  355.4 136.2 %reduce-scatter.11.cloned.1.call-start = ((), (), s32[]{:S(2)}) async-start(), calls=%async_computation.11 | async-start | bytes 4718592 | tf_op jit(solution)/shard_map/reduce_scatter | solution.py:58
  401.8 2.0 copy-start.2
  401.9 107.4 %reduce-scatter.23.cloned.1.call-start = ((), (), s32[]{:S(2)}) async-start(), calls=%async_computation.19 | async-start | bytes 7077888 | tf_op jit(solution)/shard_map/reduce_scatter | solution.py:68
  412.8 1.9 copy-start.1
  412.9 116.1 %reduce-scatter.21.cloned.1.call-start = ((), (), s32[]{:S(2)}) async-start(), calls=%async_computation.18 | async-start | bytes 7077888 | tf_op jit(solution)/shard_map/reduce_scatter | solution.py:64
  423.3 158.8 %reduce-scatter.19.cloned.1.call-start = ((), (), s32[]{:S(2)}) async-start(), calls=%async_computation.17 | async-start | bytes 1769472 | tf_op jit(solution)/shard_map/reduce_scatter | solution.py:59
  442.4 187.3 %reduce-scatter.13.cloned.1.call-start = ((), (), s32[]{:S(2)}) async-start(), calls=%async_computation.12 | async-start | bytes 1769472 | tf_op jit(solution)/shard_map/reduce_scatter | solution.py:59
  509.3 38.9 %collective-permute-start.3 = (bf16[1536,768]{1,0:T(8,128)(2,1)}, bf16[1536,768]{1,0:T(8,128)(2,1)S(1)}, u32[]{:S(2)}, u32[]{:S(2)}) collective-permute-start(bf16[1536,768]{1,0:T(8,128)(2,1)} %reduce-scatter.23.cloned.1.call-done), channel_id=1, source_target_pairs={{0,0},{1,16},{16,1},{17,17},{2,2},{3,18},{18,3},{19,19},{4,4},{5,2... | collective-permute-start | bytes 7077896 | tf_op jit(solution)/shard_map/ppermute | solution.py:71
  528.9 21.8 %collective-permute-start.2 = (bf16[768,1536]{0,1:T(8,128)(2,1)}, bf16[768,1536]{0,1:T(8,128)(2,1)}, u32[]{:S(2)}, u32[]{:S(2)}) collective-permute-start(bf16[768,1536]{0,1:T(8,128)(2,1)} %reduce-scatter.21.cloned.1.call-done), channel_id=1, source_target_pairs={{0,0},{1,16},{16,1},{17,17},{2,2},{3,18},{18,3},{19,19},{4,4},{5,2... | collective-permute-start | bytes 7077896 | tf_op jit(solution)/shard_map/ppermute | solution.py:67
Sparse Core Ops, SparseCore 0:
  18.1 98.4 all-gather.4
  118.2 92.3 all-gather.8
  213.6 41.6 reduce-scatter.8
  260.8 38.0 reduce-scatter.14
  302.3 42.9 all-gather.10
  347.4 44.2 all-gather.6
  394.1 48.2 reduce-scatter.16
  444.8 46.8 reduce-scatter.10
  494.6 14.6 reduce-scatter.22
  512.3 16.6 reduce-scatter.20
  531.9 50.1 reduce-scatter.18
  585.0 44.6 reduce-scatter.12

commit v2 on v1

v2 whole, which is shorter than its diff:
```python
import functools

import jax
import jax.numpy as jnp
from jax import lax
from jax.experimental import pallas as pl
from jax.experimental.pallas import tpu as pltpu
from jax.sharding import Mesh, PartitionSpec as P

ROOT_HALF = 0.7071067811865476
DENSITY = 0.3989422804014327
AXES = ("z", "yh", "x", "yl", "dp")
BF, F32 = jnp.bfloat16, jnp.float32

NP = 2
TB = 64
TP = 8 * TB
DB = 768
HB = 1536
CH = 256
NCH = HB // CH
NIT = NP * NCH
SLOTS = 6
ZB = TP // 4
TH = TB // 2
AG_STEPS = 5
RS_STEPS = 5
LAG = 4


def nt(a, b):
    return lax.dot_general(a, b, (((1,), (1,)), ((), ())), preferred_element_type=F32)


def tn(a, b):
    return lax.dot_general(a, b, (((0,), (0,)), ((), ())), preferred_element_type=F32)


def nn(a, b):
    return jnp.dot(a, b, preferred_element_type=F32)


def kernel(
    tok, cot, w1, w2, mlp, ig, ug, dg,
    xg, gg, w1c, w2c, ph, r1, r2, ab, yacc, dacc, py, e1, e2, f1, f2,
    st1, st2, rt1, rt2, ow1, ow2,
    own_sem, wl_sem, ws_sem, wr_sem, as_sem, ar_sem,
    zs_sem, zr_sem, gs_sem, gr_sem, ps_sem, pr_sem, ds_sem, dr_sem, os_sem, or_sem,
):
    z, yh, x, yl, k = (lax.axis_index(a) for a in AXES)
    y = yh * 2 + yl

    def up(v, n):
        return lax.rem(v + n, 4)

    z1, z2, z3 = up(z, 1), up(z, 2), up(z, 3)
    x1, x2, x3 = up(x, 1), up(x, 2), up(x, 3)
    y1, y3 = up(y, 1), up(y, 3)
    yh1, yl1, yh3, yl3 = y1 // 2, lax.rem(y1, 2), y3 // 2, lax.rem(y3, 2)
    yo, ko = 1 - yh, 1 - k
    z_dev = ((z1, yh, x, yl, k), (z3, yh, x, yl, k))
    x_dev = ((z, yh, x1, yl, k), (z, yh, x3, yl, k))
    y_dev = ((z, yh1, x, yl1, k), (z, yh3, x, yl3, k))
    far = (z, yo, x, yl, k)
    sib = (z, yh, x, yl, ko)
    diag = (z, yo, x, yl, ko)

    def send(src, dst, s_sem, r_sem, device):
        return pltpu.make_async_remote_copy(
            src_ref=src, dst_ref=dst, send_sem=s_sem, recv_sem=r_sem,
            device_id=device, device_id_type=pl.DeviceIdType.MESH,
        )

    def own(p):
        rows = pl.ds(p * TB, TB)
        return (
            pltpu.make_async_copy(tok.at[rows], xg.at[yh, p, x, yl], own_sem.at[p, 0]),
            pltpu.make_async_copy(cot.at[rows], gg.at[yh, p, x, yl], own_sem.at[p, 1]),
        )

    def hidden_at(half, c):
        return pl.multiple_of(half * HB + c * CH, CH)

    def w_own(c):
        return (
            pltpu.make_async_copy(w1.at[:, pl.ds(hidden_at(yh, c), CH)], w1c.at[c, yh], wl_sem.at[c, 0]),
            pltpu.make_async_copy(w2.at[pl.ds(hidden_at(yh, c), CH)], w2c.at[c, yh], wl_sem.at[c, 1]),
        )

    r_half = pl.ds(pl.multiple_of(k * (DB // 2), DB // 2), DB // 2)
    h_half = pl.ds(pl.multiple_of(k * (CH // 2), CH // 2), CH // 2)

    def w_far(c):
        rows = pl.ds(pl.multiple_of(yo * HB + c * CH + k * (CH // 2), CH // 2), CH // 2)
        return (
            send(w1.at[r_half, pl.ds(hidden_at(yo, c), CH)], w1c.at[c, yh, r_half],
                 ws_sem.at[c, 0, 0], wr_sem.at[c, 0, 0], far),
            send(w2.at[rows], w2c.at[c, yh, h_half], ws_sem.at[c, 0, 1], wr_sem.at[c, 0, 1], far),
        )

    def w_sib(c):
        return tuple(
            send(ref.at[c, yo, part], ref.at[c, yo, part], ws_sem.at[c, 1, a], wr_sem.at[c, 1, a], sib)
            for a, (ref, part) in enumerate(((w1c, r_half), (w2c, h_half)))
        )

    def ag(p, s):
        if s == 0:
            pairs = [[xg.at[yh, p, x, yl]] * 2, [gg.at[yh, p, x, yl]] * 2]
        elif s == 1:
            pairs = [
                [xg.at[yh, p, x3, yl, pl.ds(0, TH)], xg.at[yh, p, x1, yl, pl.ds(TH, TH)]],
                [gg.at[yh3, p, x, yl3, pl.ds(0, TH)], gg.at[yh1, p, x, yl1, pl.ds(TH, TH)]],
            ]
        elif s == 2:
            pairs = [[xg.at[yh, p, :, yl]] * 2, [gg.at[:, p, x]] * 2]
        else:
            pairs = [
                [xg.at[yh3, p, pl.ds(0, 2), yl3], xg.at[yh1, p, pl.ds(2, 2), yl1]],
                [gg.at[0, p, x3], gg.at[1, p, x1]],
            ]
        over = (x_dev, y_dev) if s < 2 else (y_dev, x_dev)
        return [
            send(pairs[a][d], pairs[a][d], as_sem.at[p, s, a, d], ar_sem.at[p, s, a, d], over[a][d])
            for a in range(2) for d in range(2)
        ]

    def ag_step(p, s):
        if s == 0:
            for copy in own(p):
                copy.wait()
        else:
            for copy in ag(p, s - 1):
                copy.wait_recv()
        if s < 4:
            for copy in ag(p, s):
                copy.start()

    def rs1(j):
        slot = lax.rem(j, SLOTS)
        return [
            send(ph.at[slot, :, z2, pl.ds(d * (ZB // 2), ZB // 2)], r1.at[j, d],
                 zs_sem.at[slot, 0, d], zr_sem.at[j, 0, d], z_dev[d])
            for d in range(2)
        ]

    def rs2(j):
        slot = lax.rem(j, SLOTS)
        return [
            send(ph.at[slot, :, (z1, z3)[d]], r2.at[j, d], zs_sem.at[slot, 1, d], zr_sem.at[j, 1, d], z_dev[d])
            for d in range(2)
        ]

    def ag1(j):
        p, c = j // NCH, lax.rem(j, NCH)
        part = ab.at[c, :, p, z]
        return [send(part, part, gs_sem.at[j, 0, d], gr_sem.at[j, 0, d], z_dev[d]) for d in range(2)]

    def ag2(j):
        p, c = j // NCH, lax.rem(j, NCH)
        parts = (
            ab.at[c, :, p, z3, pl.ds(0, ZB // 2)],
            ab.at[c, :, p, z1, pl.ds(ZB // 2, ZB // 2)],
        )
        return [
            send(parts[d], parts[d], gs_sem.at[j, 1, d], gr_sem.at[j, 1, d], z_dev[d]) for d in range(2)
        ]

    def start_item(j):
        p, c = j // NCH, lax.rem(j, NCH)
        slot = lax.rem(j, SLOTS)

        @pl.when(p == 0)
        def _():
            for copy in w_own(c):
                copy.wait()
            for copy in w_sib(c):
                copy.wait_recv()

        @pl.when(j >= SLOTS)
        def _():
            for copy in rs1(j - SLOTS) + rs2(j - SLOTS):
                copy.wait_send()

        h = nn(xg[0, p].reshape(TP, DB), w1c[c, 0])
        h = h + nn(xg[1, p].reshape(TP, DB), w1c[c, 1])
        ph[slot, 0] = h.astype(BF).reshape(4, ZB, CH)
        s = nt(gg[0, p].reshape(TP, DB), w2c[c, 0])
        s = s + nt(gg[1, p].reshape(TP, DB), w2c[c, 1])
        ph[slot, 1] = s.astype(BF).reshape(4, ZB, CH)
        for copy in rs1(j):
            copy.start()

    def merge_item(j):
        slot = lax.rem(j, SLOTS)
        for d, (copy, go) in enumerate(zip(rs1(j), rs2(j))):
            copy.wait_recv()
            rows = pl.ds(d * (ZB // 2), ZB // 2)
            to = (z1, z3)[d]
            ph[slot, :, to, rows] = (
                ph[slot, :, to, rows].astype(F32) + r1[j, d].astype(F32)
            ).astype(BF)
            go.start()

    def gelu_item(j):
        p, c = j // NCH, lax.rem(j, NCH)
        slot = lax.rem(j, SLOTS)
        for copy in rs2(j):
            copy.wait_recv()
        pre = ph[slot, 0, z].astype(F32) + r2[j, 0, 0].astype(F32) + r2[j, 1, 0].astype(F32)
        back = ph[slot, 1, z].astype(F32) + r2[j, 0, 1].astype(F32) + r2[j, 1, 1].astype(F32)
        cdf = 0.5 * (1.0 + lax.erf(pre * ROOT_HALF))
        ab[c, 0, p, z] = (pre * cdf).astype(BF)
        ab[c, 1, p, z] = (back * (cdf + pre * DENSITY * jnp.exp(-0.5 * pre * pre))).astype(BF)
        for copy in ag1(j):
            copy.start()

    def spread_item(j):
        for copy, go in zip(ag1(j), ag2(j)):
            copy.wait_recv()
            go.start()

    def to_sib(c):
        slot = lax.rem(c, 2)
        return (
            send(st1.at[slot], rt1.at[c], ds_sem.at[slot, 0], dr_sem.at[c, 0], sib),
            send(st2.at[slot], rt2.at[c], ds_sem.at[slot, 1], dr_sem.at[c, 1], sib),
        )

    def out_parts(c):
        hid = pl.ds(pl.multiple_of(c * CH, CH), CH)
        return ((rt1.at[c], ug.at[:, hid]), (rt2.at[c], dg.at[hid]))

    def out_local(c):
        return [pltpu.make_async_copy(s, d, os_sem.at[c, a]) for a, (s, d) in enumerate(out_parts(c))]

    def out_far(c):
        return [send(s, d, os_sem.at[c, a], or_sem.at[c, a], diag) for a, (s, d) in enumerate(out_parts(c))]

    def use_item(j):
        p, c = j // NCH, lax.rem(j, NCH)
        for copy in ag2(j):
            copy.wait_recv()
        act = ab[c, 0, p].reshape(TP, CH)
        hid = ab[c, 1, p].reshape(TP, CH)

        @pl.when(c == 0)
        def _():
            for half in range(2):
                yacc[half] = nn(act, w2c[c, half])
                dacc[half] = nt(hid, w1c[c, half])

        @pl.when(c > 0)
        def _():
            for half in range(2):
                yacc[half] += nn(act, w2c[c, half])
                dacc[half] += nt(hid, w1c[c, half])

        @pl.when(p == NP - 1)
        def _():
            slot = lax.rem(c, 2)

            @pl.when(c >= 2)
            def _():
                for copy in to_sib(c - 2):
                    copy.wait_send()

            acts = ab[c, 0].reshape(NP * TP, CH)
            hids = ab[c, 1].reshape(NP * TP, CH)
            st1[slot] = tn(xg[ko].reshape(NP * TP, DB), hids).astype(BF)
            st2[slot] = tn(acts, gg[ko].reshape(NP * TP, DB)).astype(BF)
            for copy in to_sib(c):
                copy.start()
            ow1[...] = tn(xg[k].reshape(NP * TP, DB), hids)
            ow2[...] = tn(acts, gg[k].reshape(NP * TP, DB))

    def finish_grad(c):
        for copy in to_sib(c):
            copy.wait_recv()
        rt1[c] = (rt1[c].astype(F32) + ow1[...]).astype(BF)
        rt2[c] = (rt2[c].astype(F32) + ow2[...]).astype(BF)

        @pl.when(k == yh)
        def _():
            for copy in out_local(c):
                copy.start()

        @pl.when(k != yh)
        def _():
            for copy in out_far(c):
                copy.start()

    def rs(p, s):
        if s == 0:
            srcs = [
                [py.at[0, 0, x2], py.at[0, 1, x2]],
                [py.at[1, yo, pl.ds(0, 2), yl], py.at[1, yo, pl.ds(2, 2), yl]],
            ]
            dsts = e1
        elif s == 1:
            srcs = [
                [py.at[0, :, x1], py.at[0, :, x3]],
                [py.at[1, yh1, :, yl1], py.at[1, yh3, :, yl3]],
            ]
            dsts = None
        elif s == 2:
            srcs = [
                [py.at[0, yo, x, yl, pl.ds(0, TH)], py.at[0, yo, x, yl, pl.ds(TH, TH)]],
                [py.at[1, yh, x2, yl, pl.ds(0, TH)], py.at[1, yh, x2, yl, pl.ds(TH, TH)]],
            ]
            dsts = f1
        else:
            srcs = [
                [py.at[0, yh1, x, yl1], py.at[0, yh3, x, yl3]],
                [py.at[1, yh, x1, yl], py.at[1, yh, x3, yl]],
            ]
            dsts = f2
        over = (x_dev, y_dev) if s < 2 else (y_dev, x_dev)
        copies = []
        for a in range(2):
            for d in range(2):
                dst = dsts.at[p, a, d] if s != 1 else (e2a, e2b)[a].at[p, d]
                copies.append(send(srcs[a][d], dst, ps_sem.at[s, a, d], pr_sem.at[p, s, a, d], over[a][d]))
        return copies

    e2a, e2b = e2

    def bump(ref, index, more):
        ref[index] = (ref[index].astype(F32) + more.astype(F32)).astype(BF)

    def rs_step(p, s):
        if s == 0:
            for half in range(2):
                py[0, half] = yacc[half].astype(BF).reshape(4, 2, TB, DB)
                py[1, half] = dacc[half].astype(BF).reshape(4, 2, TB, DB)
        else:
            for copy in rs(p, s - 1):
                copy.wait_recv()
        if s == 1:
            bump(py, (0, 0, x1), e1[p, 0, 0])
            bump(py, (0, 1, x3), e1[p, 0, 1])
            bump(py, (1, yh1, pl.ds(0, 2), yl1), e1[p, 1, 0])
            bump(py, (1, yh3, pl.ds(2, 2), yl3), e1[p, 1, 1])
        elif s == 2:
            for half in range(2):
                py[0, half, x] = (
                    py[0, half, x].astype(F32) + e2a[p, 0, half].astype(F32) + e2a[p, 1, half].astype(F32)
                ).astype(BF)
            for at in range(4):
                py[1, yh, at, yl] = (
                    py[1, yh, at, yl].astype(F32) + e2b[p, 0, at].astype(F32) + e2b[p, 1, at].astype(F32)
                ).astype(BF)
        elif s == 3:
            low, high = pl.ds(0, TH), pl.ds(TH, TH)
            bump(py, (0, yh1, x, yl1, low), f1[p, 0, 0])
            bump(py, (0, yh3, x, yl3, high), f1[p, 0, 1])
            bump(py, (1, yh, x1, yl, low), f1[p, 1, 0])
            bump(py, (1, yh, x3, yl, high), f1[p, 1, 1])
        elif s == 4:
            rows = pl.ds(pl.multiple_of(p * TB, TB), TB)
            for a, out in enumerate((mlp, ig)):
                out[rows] = (
                    py[a, yh, x, yl].astype(F32) + f2[p, a, 0].astype(F32) + f2[p, a, 1].astype(F32)
                ).astype(BF)
            for at in range(4):
                for copy in rs(p, at):
                    copy.wait_send()
        if s < 4:
            for copy in rs(p, s):
                copy.start()

    barrier = pltpu.get_barrier_semaphore()
    peers = (*z_dev, *x_dev, *y_dev, far, sib, diag)
    for p in range(NP):
        for copy in own(p):
            copy.start()
    for c in range(NCH):
        for copy in w_own(c):
            copy.start()
    for device in peers:
        pl.semaphore_signal(barrier, inc=1, device_id=device, device_id_type=pl.DeviceIdType.MESH)
    pl.semaphore_wait(barrier, len(peers))

    for copy in w_far(0):
        copy.start()

    first = -AG_STEPS
    last = NIT + LAG - 1 + RS_STEPS

    def step(it, carry):
        i = it + first
        for s in range(AG_STEPS):
            @pl.when((lax.rem(it, AG_STEPS) == s) & (it < NP * AG_STEPS))
            def _():
                ag_step(it // AG_STEPS, s)

        @pl.when((i + 3 >= 1) & (i + 3 < NCH))
        def _():
            for copy in w_far(i + 3):
                copy.start()

        @pl.when((i + 1 >= 0) & (i + 1 < NCH))
        def _():
            for copy, go in zip(w_far(i + 1), w_sib(i + 1)):
                copy.wait_recv()
                go.start()

        @pl.when((i >= 1) & (i - 1 < NIT))
        def _():
            merge_item(i - 1)

        @pl.when((i >= 2) & (i - 2 < NIT))
        def _():
            gelu_item(i - 2)

        @pl.when((i >= 3) & (i - 3 < NIT))
        def _():
            spread_item(i - 3)

        @pl.when((i - LAG - 1 >= NIT - NCH) & (i - LAG - 1 < NIT))
        def _():
            finish_grad(i - LAG - 1 - (NIT - NCH))

        @pl.when((i >= 0) & (i < NIT))
        def _():
            start_item(i)

        @pl.when((i >= LAG) & (i - LAG < NIT))
        def _():
            use_item(i - LAG)

        q = i - (LAG + NCH - 1)
        for s in range(RS_STEPS):
            @pl.when((q >= 0) & (lax.rem(q + 2 * NCH, NCH) == s))
            def _():
                rs_step(q // NCH, s)

        return carry

    lax.fori_loop(0, last - first, step, 0)

    for p in range(NP):
        for s in range(4):
            for copy in ag(p, s):
                copy.wait_send()

    def drain(j, carry):
        for copy in ag1(j) + ag2(j):
            copy.wait_send()

        @pl.when(j >= NIT - SLOTS)
        def _():
            for copy in rs1(j) + rs2(j):
                copy.wait_send()

        @pl.when(j < NCH)
        def _():
            for copy in w_far(j) + w_sib(j):
                copy.wait_send()

            @pl.when(j >= NCH - 2)
            def _():
                for copy in to_sib(j):
                    copy.wait_send()

            @pl.when(k == yh)
            def _():
                for copy in out_local(j):
                    copy.wait()

            @pl.when(k != yh)
            def _():
                for copy in out_far(j):
                    copy.wait()

        return carry

    lax.fori_loop(0, NIT, drain, 0)


def on_device(tokens, up_weight, down_weight, cotangent):
    vmem, dma = pltpu.VMEM, pltpu.SemaphoreType.DMA
    anywhere = pl.BlockSpec(memory_space=pl.ANY)
    inside = pl.BlockSpec(memory_space=pltpu.VMEM)

    def body(*refs):
        refs = list(refs)
        at = 8 + 12
        kernel(*refs[:at], (refs[at], refs[at + 1]), *refs[at + 2:])

    mlp, ig, ug, dg = pl.pallas_call(
        body,
        out_shape=(
            jax.ShapeDtypeStruct((NP * TB, DB), BF),
            jax.ShapeDtypeStruct((NP * TB, DB), BF),
            jax.ShapeDtypeStruct((DB, HB), BF),
            jax.ShapeDtypeStruct((HB, DB), BF),
        ),
        in_specs=[anywhere] * 4,
        out_specs=(inside, inside, anywhere, anywhere),
        scratch_shapes=[
            vmem((2, NP, 4, 2, TB, DB), BF),
            vmem((2, NP, 4, 2, TB, DB), BF),
            vmem((NCH, 2, DB, CH), BF),
            vmem((NCH, 2, CH, DB), BF),
            vmem((SLOTS, 2, 4, ZB, CH), BF),
            vmem((NIT, 2, 2, ZB // 2, CH), BF),
            vmem((NIT, 2, 2, ZB, CH), BF),
            vmem((NCH, 2, NP, 4, ZB, CH), BF),
            vmem((2, TP, DB), F32),
            vmem((2, TP, DB), F32),
            vmem((2, 2, 4, 2, TB, DB), BF),
            vmem((NP, 2, 2, 2, TB, DB), BF),
            vmem((NP, 2, 2, 2, TB, DB), BF),
            vmem((NP, 2, 4, TB, DB), BF),
            vmem((NP, 2, 2, TH, DB), BF),
            vmem((NP, 2, 2, TB, DB), BF),
            vmem((2, DB, CH), BF),
            vmem((2, CH, DB), BF),
            vmem((NCH, DB, CH), BF),
            vmem((NCH, CH, DB), BF),
            vmem((DB, CH), F32),
            vmem((CH, DB), F32),
            dma((NP, 2)),
            dma((NCH, 2)),
            dma((NCH, 2, 2)),
            dma((NCH, 2, 2)),
            dma((NP, 4, 2, 2)),
            dma((NP, 4, 2, 2)),
            dma((SLOTS, 2, 2)),
            dma((NIT, 2, 2)),
            dma((NIT, 2, 2)),
            dma((NIT, 2, 2)),
            dma((4, 2, 2)),
            dma((NP, 4, 2, 2)),
            dma((2, 2)),
            dma((NCH, 2)),
            dma((NCH, 2)),
            dma((NCH, 2)),
        ],
        compiler_params=pltpu.CompilerParams(
            collective_id=0, has_side_effects=True, vmem_limit_bytes=62 * 2**20
        ),
        cost_estimate=pl.CostEstimate(flops=29 * 10**9, bytes_accessed=20 * 10**6, transcendentals=10**6),
        name="block",
    )(tokens, cotangent, up_weight, down_weight)
    return mlp, ig, ug.astype(F32), dg.astype(F32)


def solution(mesh):
    fine = Mesh(mesh.devices.reshape(4, 2, 4, 2, 2), AXES)
    rows = P(("dp", "x", "yl"), ("z", "yh"))
    return jax.shard_map(
        on_device,
        mesh=fine,
        in_specs=(rows, P(("z", "yh"), ("x", "yl")), P(("x", "yl"), ("z", "yh")), rows),
        out_specs=(rows, rows, P(("z", "yh"), ("x", "yl", "dp")), P(("x", "yl", "dp"), ("z", "yh"))),
        check_vma=False,
    )
```

time: 639 us -> 288 us (0.45)
  waiting for transfers between devices: 498 us -> 0 us
  Pallas kernels: 0 us -> 279 us
  matrix products: 57.3 us -> 0 us
  starting transfers between devices: 24.9 us -> 0 us
  blocking collectives: 19.3 us -> 0 us
  local copies, waits for them, and re-layouts: 16.5 us -> 1.37 us
  between operations: 14.2 us -> 0.65 us
    pallas_call x0 -> x1, Pallas kernels: none -> 279 us  [on_device(): pl.pallas_call(body, out_shape=(jax.ShapeDtypeStruct((NP * TB, DB), BF),...]
    reduce_scatter x8 -> x0, waiting for transfers between devices: 216 us -> none  [the longest x2 74.3 us: spread(): return lax.psum_scatter(part, ('x', 'yl'), scatter_dimension=0, tiled=True)]
    ppermute x4 -> x0, waiting for transfers between devices: 203 us -> none  [the longest x1 125 us: on_device(): lax.ppermute(lax.dynamic_slice_in_dim(up_weight, (1 - yh) * half, half, 1...]
    all_gather x4 -> x0, waiting for transfers between devices: 78.6 us -> none  [the longest x1 42.3 us: on_device(): hidden_grad = lax.all_gather(hidden_grad, 'z', axis=0, tiled=True)]
    dot_general x6 -> x0, matrix products: 57.3 us -> none  [the longest x2 20.5 us: contract_last(): lax.dot_general(matrix_a, matrix_b, (((1,), (1,)), ((), ())), preferred_e...]
    ppermute x4 -> x0, starting transfers between devices: 24.1 us -> none  [the longest x1 19.3 us: on_device(): up_grad = lax.ppermute(up_grad, ('yh', 'dp'), across)]
    all_gather x2 -> x0, blocking collectives: 19.3 us -> none  [on_device(): lax.all_gather(part, 'yh', axis=1, tiled=True)]
    dynamic_slice x2 -> x0, local copies, waits for them, and re-layouts: 8.34 us -> none  [the longest x1 4.22 us: on_device(): up_mine = lax.dynamic_slice_in_dim(up_weight, yh * half, half, 1)]
  transfers between devices with their start and end apart: 16 -> 0, of which waited for: 11 -> 0; matrix products, arithmetic and copies ran while one was open for 11% -> 0% of each run, Pallas kernels for 0% -> 0%
where the time goes in v2:
time: 288 us
  Pallas kernels  279 us (97%)
  other arithmetic  7.19 us (2%)
    pallas_call x1, Pallas kernels, on_device(): pl.pallas_call(body, out_shape=(jax.ShapeDtypeStruct((NP * TB, DB), BF),...  279 us
    convert_element_type x2, other arithmetic, on_device(): return (mlp, ig, ug.astype(F32), dg.astype(F32))  7.19 us

profile of v2, /device:TPU:0, one launch (start us, length us, event | category | flops | bytes accessed | tf_op | source)
XLA Modules:
  0.0 288.1 jit_solution(1009365432127506841)
XLA Ops:
  0.6 278.9 %block.1 = (bf16[128,768]{1,0:T(8,128)(2,1)}, bf16[128,768]{1,0:T(8,128)(2,1)}, bf16[768,1536]{1,0:T(8,128)(2,1)}, bf16[1536,768]{1,0:T(8,128)(2,1)}) custom-call(bf16[128,768]{1,0:T(8,128)(2,1)} %refs_0_.1, bf16[128,768]{1,0:T(8,128)(2,1)} %refs_1_.1, bf16[768,3072]{1,0:T(8,128)(2,1)} %refs_2_.1, bf16[3072,768]{1,0:T(8,128)(2,1)} %refs_3_.1), custom_call_target="tpu_custom_call" | custom-call | flops 28999999488 | bytes 20000000 | tf_op jit(solution)/shard_map/block/pallas_call | solution.py:491
  279.5 0.0 copy-start
  279.6 4.6 %convert_element_type.6 = f32[768,1536]{1,0:T(8,128)} convert(bf16[768,1536]{1,0:T(8,128)(2,1)} %get-tuple-element.10) | non-fusion elementwise | flops 1179648 | bytes 7077888 | tf_op jit(solution)/shard_map/convert_element_type | solution.py:547
  284.2 0.0 copy-done
  284.2 0.0 copy-start.2
  284.2 0.0 copy-start.1
  284.2 2.5 convert_element_type.7
  286.8 0.0 copy-done.2
  286.8 0.7 copy.10
  287.4 0.0 copy-done.1
  287.4 0.7 copy.11
Async XLA Ops:
  279.5 4.7 %copy-start = (bf16[1536,768]{1,0:T(8,128)(2,1)S(1)}, bf16[1536,768]{1,0:T(8,128)(2,1)}, u32[]{:S(2)}) copy-start(bf16[1536,768]{1,0:T(8,128)(2,1)} %get-tuple-element.11) | copy-start | bytes 7077892
  284.2 2.6 copy-start.2
  284.2 3.2 %copy-start.1 = (bf16[128,768]{1,0:T(8,128)(2,1)S(1)}, bf16[128,768]{1,0:T(8,128)(2,1)}, u32[]{:S(2)}) copy-start(bf16[128,768]{1,0:T(8,128)(2,1)} %get-tuple-element.17) | copy-start | bytes 589828

commit v3 on v2

v3 whole, which is shorter than its diff:
```python
import functools

import jax
import jax.numpy as jnp
from jax import lax
from jax.experimental import pallas as pl
from jax.experimental.pallas import tpu as pltpu
from jax.sharding import Mesh, PartitionSpec as P

ROOT_HALF = 0.7071067811865476
DENSITY = 0.3989422804014327
AXES = ("z", "yh", "x", "yl", "dp")
BF, F32 = jnp.bfloat16, jnp.float32

NP = 4
AS = 2
TB = 32
TP = 8 * TB
DB = 768
HB = 1536
CH = 256
NCH = HB // CH
NIT = NP * NCH
ZB = TP // 4
TH = TB // 2
OPS = (
    "start", "merge", "gelu", "spread", "use", "w_far0", "w_far1", "w_sib0", "w_sib1", "w_wait",
    "ag0", "ag1", "ag2", "ag3", "ag_wait", "rs0", "rs1", "rs2", "rs3", "rs4", "dw", "fin", "nop",
)
STEPS = (
    320, 321, 160, 352, 353, 323, 192, 384, 355, 224, 322, 197, 385, 256, 165, 416,
    417, 354, 261, 288, 387, 161, 229, 386, 325, 448, 0, 193, 293, 5, 32, 419,
    324, 162, 37, 225, 418, 64, 257, 356, 69, 357, 194, 289, 449, 96, 11, 1,
    7, 164, 101, 6, 326, 43, 388, 33, 39, 38, 258, 327, 196, 226, 389, 75,
    65, 290, 8, 2, 228, 359, 70, 195, 71, 97, 421, 260, 34, 40, 420, 163,
    103, 102, 292, 10, 4, 66, 391, 259, 358, 128, 450, 107, 72, 227, 42, 134,
    98, 390, 36, 291, 3, 104, 9, 74, 423, 129, 35, 422, 68, 130, 41, 12,
    67, 133, 13, 100, 451, 19, 18, 99, 20, 44, 14, 132, 50, 131, 481, 106,
    73, 76, 480, 82, 51, 513, 135, 138, 105, 45, 139, 136, 108, 512, 114, 15,
    83, 137, 46, 77, 483, 140, 482, 146, 52, 640, 545, 115, 17, 544, 78, 109,
    21, 47, 84, 577, 147, 576, 672, 49, 515, 141, 641, 110, 16, 53, 116, 514,
    79, 81, 608, 142, 609, 547, 673, 48, 148, 85, 642, 111, 22, 546, 80, 117,
    23, 54, 113, 579, 674, 143, 112, 149, 55, 643, 86, 145, 144, 485, 87, 118,
    484, 578, 675, 119, 517, 150, 644, 611, 151, 516, 610, 487, 549, 676, 645, 486,
    519, 548, 677, 518, 551, 550, 580, 581, 583, 582, 613, 615, 612, 614,
)


def nt(a, b):
    return lax.dot_general(a, b, (((1,), (1,)), ((), ())), preferred_element_type=F32)


def tn(a, b):
    return lax.dot_general(a, b, (((0,), (0,)), ((), ())), preferred_element_type=F32)


def nn(a, b):
    return jnp.dot(a, b, preferred_element_type=F32)


def kernel(
    tok, cot, w1, w2, mlp, ig, ug, dg,
    tg, w1c, w2c, ph, r1, r2, ab, acc, py, e1, e2, f1, f2, st1, st2, rt1, rt2, ow1, ow2,
    own_sem, wl_sem, ws_sem, wr_sem, as_sem, ar_sem,
    zs_sem, zr_sem, gs_sem, gr_sem, ps_sem, pr_sem, ds_sem, dr_sem, os_sem, or_sem,
):
    z, yh, x, yl, k = (lax.axis_index(a) for a in AXES)
    y = yh * 2 + yl

    def up(v, n):
        return lax.rem(v + n, 4)

    z1, z2, z3 = up(z, 1), up(z, 2), up(z, 3)
    x1, x2, x3 = up(x, 1), up(x, 2), up(x, 3)
    y1, y3 = up(y, 1), up(y, 3)
    yh1, yl1, yh3, yl3 = y1 // 2, lax.rem(y1, 2), y3 // 2, lax.rem(y3, 2)
    yo, ko = 1 - yh, 1 - k
    z_dev = ((z1, yh, x, yl, k), (z3, yh, x, yl, k))
    x_dev = ((z, yh, x1, yl, k), (z, yh, x3, yl, k))
    y_dev = ((z, yh1, x, yl1, k), (z, yh3, x, yl3, k))
    far = (z, yo, x, yl, k)
    sib = (z, yh, x, yl, ko)
    diag = (z, yo, x, yl, ko)

    def send(src, dst, s_sem, r_sem, device):
        return pltpu.make_async_remote_copy(
            src_ref=src, dst_ref=dst, send_sem=s_sem, recv_sem=r_sem,
            device_id=device, device_id_type=pl.DeviceIdType.MESH,
        )

    def own(p, a):
        rows = pl.ds(pl.multiple_of(p * TB, TB), TB)
        return pltpu.make_async_copy((tok, cot)[a].at[rows], tg.at[a, yh, p, x, yl], own_sem.at[p, a])

    def hidden_at(half, c):
        return pl.multiple_of(half * HB + c * CH, CH)

    def w_own(c):
        return (
            pltpu.make_async_copy(w1.at[:, pl.ds(hidden_at(yh, c), CH)], w1c.at[c, yh], wl_sem.at[c, 0]),
            pltpu.make_async_copy(w2.at[pl.ds(hidden_at(yh, c), CH)], w2c.at[c, yh], wl_sem.at[c, 1]),
        )

    r_half = pl.ds(pl.multiple_of(k * (DB // 2), DB // 2), DB // 2)
    h_half = pl.ds(pl.multiple_of(k * (CH // 2), CH // 2), CH // 2)

    def w_far(c):
        rows = pl.ds(pl.multiple_of(yo * HB + c * CH + k * (CH // 2), CH // 2), CH // 2)
        return (
            send(w1.at[r_half, pl.ds(hidden_at(yo, c), CH)], w1c.at[c, yh, r_half],
                 ws_sem.at[c, 0, 0], wr_sem.at[c, 0, 0], far),
            send(w2.at[rows], w2c.at[c, yh, h_half], ws_sem.at[c, 0, 1], wr_sem.at[c, 0, 1], far),
        )

    def w_sib(c):
        return tuple(
            send(ref.at[c, yo, part], ref.at[c, yo, part], ws_sem.at[c, 1, a], wr_sem.at[c, 1, a], sib)
            for a, (ref, part) in enumerate(((w1c, r_half), (w2c, h_half)))
        )

    def ag(s, p, a):
        over = (y_dev, x_dev)[s // 2]
        if s == 0:
            parts = [tg.at[a, yh, p, x, yl]] * 2
        elif s == 1:
            parts = [tg.at[a, yh3, p, x, yl3, pl.ds(0, TH)], tg.at[a, yh1, p, x, yl1, pl.ds(TH, TH)]]
        elif s == 2:
            parts = [tg.at[a, :, p, x]] * 2
        else:
            parts = [tg.at[a, 0, p, x3], tg.at[a, 1, p, x1]]
        return [
            send(parts[d], parts[d], as_sem.at[p, s, a, d], ar_sem.at[p, s, a, d], over[d]) for d in range(2)
        ]

    def ag_step(s, arg):
        p, a = arg // 2, lax.rem(arg, 2)
        if s == 0:
            for b in range(2):
                @pl.when(a == b)
                def _():
                    own(p, b).wait()
        else:
            for copy in ag(s - 1, p, a):
                copy.wait_recv()
        for copy in ag(s, p, a):
            copy.start()

    def ag_wait(p):
        for a in range(2):
            for copy in ag(3, p, a):
                copy.wait_recv()

    def rs1(j):
        return [
            send(ph.at[j, :, z2, pl.ds(d * (ZB // 2), ZB // 2)], r1.at[j, d],
                 zs_sem.at[j, 0, d], zr_sem.at[j, 0, d], z_dev[d])
            for d in range(2)
        ]

    def rs2(j):
        return [
            send(ph.at[j, :, (z1, z3)[d]], r2.at[j, d], zs_sem.at[j, 1, d], zr_sem.at[j, 1, d], z_dev[d])
            for d in range(2)
        ]

    def ag1(j):
        p, c = j // NCH, lax.rem(j, NCH)
        part = ab.at[c, :, p, z]
        return [send(part, part, gs_sem.at[j, 0, d], gr_sem.at[j, 0, d], z_dev[d]) for d in range(2)]

    def ag2(j):
        p, c = j // NCH, lax.rem(j, NCH)
        parts = (
            ab.at[c, :, p, z3, pl.ds(0, ZB // 2)],
            ab.at[c, :, p, z1, pl.ds(ZB // 2, ZB // 2)],
        )
        return [
            send(parts[d], parts[d], gs_sem.at[j, 1, d], gr_sem.at[j, 1, d], z_dev[d]) for d in range(2)
        ]

    def start_item(j):
        p, c = j // NCH, lax.rem(j, NCH)
        h = nn(tg[0, 0, p].reshape(TP, DB), w1c[c, 0])
        h = h + nn(tg[0, 1, p].reshape(TP, DB), w1c[c, 1])
        ph[j, 0] = h.astype(BF).reshape(4, ZB, CH)
        s = nt(tg[1, 0, p].reshape(TP, DB), w2c[c, 0])
        s = s + nt(tg[1, 1, p].reshape(TP, DB), w2c[c, 1])
        ph[j, 1] = s.astype(BF).reshape(4, ZB, CH)
        for copy in rs1(j):
            copy.start()

    def merge_item(j):
        for d, (copy, go) in enumerate(zip(rs1(j), rs2(j))):
            copy.wait_recv()
            rows = pl.ds(d * (ZB // 2), ZB // 2)
            to = (z1, z3)[d]
            ph[j, :, to, rows] = (
                ph[j, :, to, rows].astype(F32) + r1[j, d].astype(F32)
            ).astype(BF)
            go.start()

    def gelu_item(j):
        p, c = j // NCH, lax.rem(j, NCH)
        for copy in rs2(j):
            copy.wait_recv()
        pre = ph[j, 0, z].astype(F32) + r2[j, 0, 0].astype(F32) + r2[j, 1, 0].astype(F32)
        back = ph[j, 1, z].astype(F32) + r2[j, 0, 1].astype(F32) + r2[j, 1, 1].astype(F32)
        cdf = 0.5 * (1.0 + lax.erf(pre * ROOT_HALF))
        ab[c, 0, p, z] = (pre * cdf).astype(BF)
        ab[c, 1, p, z] = (back * (cdf + pre * DENSITY * jnp.exp(-0.5 * pre * pre))).astype(BF)
        for copy in ag1(j):
            copy.start()

    def spread_item(j):
        for copy, go in zip(ag1(j), ag2(j)):
            copy.wait_recv()
            go.start()

    def to_sib(c):
        slot = lax.rem(c, 2)
        return (
            send(st1.at[slot], rt1.at[c], ds_sem.at[slot, 0], dr_sem.at[c, 0], sib),
            send(st2.at[slot], rt2.at[c], ds_sem.at[slot, 1], dr_sem.at[c, 1], sib),
        )

    def out_parts(c):
        hid = pl.ds(pl.multiple_of(c * CH, CH), CH)
        return ((rt1.at[c], ug.at[:, hid]), (rt2.at[c], dg.at[hid]))

    def out_local(c):
        return [pltpu.make_async_copy(s, d, os_sem.at[c, a]) for a, (s, d) in enumerate(out_parts(c))]

    def out_far(c):
        return [send(s, d, os_sem.at[c, a], or_sem.at[c, a], diag) for a, (s, d) in enumerate(out_parts(c))]

    def use_item(j):
        p, c = j // NCH, lax.rem(j, NCH)
        for copy in ag2(j):
            copy.wait_recv()
        act = ab[c, 0, p].reshape(TP, CH)
        hid = ab[c, 1, p].reshape(TP, CH)
        slot = lax.rem(p, AS)

        @pl.when(c == 0)
        def _():
            for half in range(2):
                acc[slot, 0, half] = nn(act, w2c[c, half])
                acc[slot, 1, half] = nt(hid, w1c[c, half])

        @pl.when(c > 0)
        def _():
            for half in range(2):
                acc[slot, 0, half] += nn(act, w2c[c, half])
                acc[slot, 1, half] += nt(hid, w1c[c, half])

    def grad_item(c):
        slot = lax.rem(c, 2)

        @pl.when(c >= 2)
        def _():
            for copy in to_sib(c - 2):
                copy.wait_send()

        acts = ab[c, 0].reshape(NP * TP, CH)
        hids = ab[c, 1].reshape(NP * TP, CH)
        st1[slot] = tn(tg[0, ko].reshape(NP * TP, DB), hids).astype(BF)
        st2[slot] = tn(acts, tg[1, ko].reshape(NP * TP, DB)).astype(BF)
        for copy in to_sib(c):
            copy.start()
        ow1[...] = tn(tg[0, k].reshape(NP * TP, DB), hids)
        ow2[...] = tn(acts, tg[1, k].reshape(NP * TP, DB))

    def finish_grad(c):
        for copy in to_sib(c):
            copy.wait_recv()
        rt1[c] = (rt1[c].astype(F32) + ow1[...]).astype(BF)
        rt2[c] = (rt2[c].astype(F32) + ow2[...]).astype(BF)

        @pl.when(k == yh)
        def _():
            for copy in out_local(c):
                copy.start()

        @pl.when(k != yh)
        def _():
            for copy in out_far(c):
                copy.start()

    def rs(s, p, a):
        over = (x_dev, y_dev)[s // 2]
        slot = lax.rem(p, AS)
        if s == 0:
            srcs = [py.at[slot, a, d, x2] for d in range(2)]
        elif s == 1:
            srcs = [py.at[slot, a, :, x1], py.at[slot, a, :, x3]]
        elif s == 2:
            srcs = [py.at[slot, a, yo, x, yl, pl.ds(d * TH, TH)] for d in range(2)]
        else:
            srcs = [py.at[slot, a, yh1, x, yl1], py.at[slot, a, yh3, x, yl3]]
        return [
            send(srcs[d], (e1, e2, f1, f2)[s].at[p, a, d], ps_sem.at[p, s, a, d], pr_sem.at[p, s, a, d], over[d])
            for d in range(2)
        ]

    def bump(ref, index, *more):
        total = ref[index].astype(F32)
        for term in more:
            total = total + term.astype(F32)
        ref[index] = total.astype(BF)

    def rs_step(s, arg):
        p, a = arg // 2, lax.rem(arg, 2)
        slot = lax.rem(p, AS)
        if s == 0:
            for half in range(2):
                py[slot, a, half] = acc[slot, a, half].astype(BF).reshape(4, 2, TB, DB)
        else:
            for copy in rs(s - 1, p, a):
                copy.wait_recv()
        if s == 1:
            bump(py, (slot, a, 0, x1), e1[p, a, 0])
            bump(py, (slot, a, 1, x3), e1[p, a, 1])
        elif s == 2:
            for half in range(2):
                bump(py, (slot, a, half, x), e2[p, a, 0, half], e2[p, a, 1, half])
        elif s == 3:
            bump(py, (slot, a, yh1, x, yl1, pl.ds(0, TH)), f1[p, a, 0])
            bump(py, (slot, a, yh3, x, yl3, pl.ds(TH, TH)), f1[p, a, 1])
        elif s == 4:
            rows = pl.ds(pl.multiple_of(p * TB, TB), TB)
            total = (
                py[slot, a, yh, x, yl].astype(F32) + f2[p, a, 0].astype(F32) + f2[p, a, 1].astype(F32)
            ).astype(BF)
            for b, out in enumerate((mlp, ig)):
                @pl.when(a == b)
                def _():
                    out[rows] = total
            for at in range(4):
                for copy in rs(at, p, a):
                    copy.wait_send()
        if s < 4:
            for copy in rs(s, p, a):
                copy.start()

    barrier = pltpu.get_barrier_semaphore()
    peers = (*z_dev, *x_dev, *y_dev, far, sib, diag)
    for p in range(NP):
        for a in range(2):
            own(p, a).start()
    for c in range(NCH):
        for copy in w_own(c):
            copy.start()
    for device in peers:
        pl.semaphore_signal(barrier, inc=1, device_id=device, device_id_type=pl.DeviceIdType.MESH)
    pl.semaphore_wait(barrier, len(peers))

    def w_far_step(a, c):
        w_far(c)[a].start()

    def w_sib_step(a, c):
        w_far(c)[a].wait_recv()
        w_sib(c)[a].start()

    def w_wait(c):
        for copy in w_own(c):
            copy.wait()
        for copy in w_sib(c):
            copy.wait_recv()

    runs = [start_item, merge_item, gelu_item, spread_item, use_item]
    runs += [functools.partial(w_far_step, a) for a in range(2)]
    runs += [functools.partial(w_sib_step, a) for a in range(2)]
    runs += [w_wait]
    runs += [functools.partial(ag_step, s) for s in range(4)]
    runs += [ag_wait]
    runs += [functools.partial(rs_step, s) for s in range(5)]
    runs += [grad_item, finish_grad]
    nop = OPS.index("nop")

    def dispatch(lo, hi, what, arg):
        if hi - lo == 1:
            if lo < nop:
                runs[lo](arg)
            return
        mid = (lo + hi) // 2

        @pl.when(what < mid)
        def _():
            dispatch(lo, mid, what, arg)

        @pl.when(what >= mid)
        def _():
            dispatch(mid, hi, what, arg)

    steps = list(STEPS) + [nop * 32] * (-len(STEPS) % 3)
    words = [steps[n] + steps[n + 1] * 1024 + steps[n + 2] * 1024 * 1024 for n in range(0, len(steps), 3)]

    def word(n, carry):
        value = jnp.int32(words[0])
        for at in range(1, len(words)):
            value = jnp.where(n == at, jnp.int32(words[at]), value)

        def step(_, left):
            now = lax.rem(left, 1024)
            dispatch(0, nop + 1, now // 32, lax.rem(now, 32))
            return left // 1024

        lax.fori_loop(0, 3, step, value)
        return carry

    lax.fori_loop(0, len(words), word, 0)

    def drain(j, carry):
        for copy in rs1(j) + rs2(j) + ag1(j) + ag2(j):
            copy.wait_send()

        @pl.when(j < NP * 2)
        def _():
            for s in range(4):
                for copy in ag(s, j // 2, lax.rem(j, 2)):
                    copy.wait_send()

        @pl.when(j < NCH)
        def _():
            for copy in w_far(j) + w_sib(j):
                copy.wait_send()

            @pl.when(j >= NCH - 2)
            def _():
                for copy in to_sib(j):
                    copy.wait_send()

            @pl.when(k == yh)
            def _():
                for copy in out_local(j):
                    copy.wait()

            @pl.when(k != yh)
            def _():
                for copy in out_far(j):
                    copy.wait()

        return carry

    lax.fori_loop(0, NIT, drain, 0)


def on_device(tokens, up_weight, down_weight, cotangent):
    vmem, dma = pltpu.VMEM, pltpu.SemaphoreType.DMA
    anywhere = pl.BlockSpec(memory_space=pl.ANY)
    inside = pl.BlockSpec(memory_space=pltpu.VMEM)

    mlp, ig, ug, dg = pl.pallas_call(
        kernel,
        out_shape=(
            jax.ShapeDtypeStruct((NP * TB, DB), BF),
            jax.ShapeDtypeStruct((NP * TB, DB), BF),
            jax.ShapeDtypeStruct((DB, HB), BF),
            jax.ShapeDtypeStruct((HB, DB), BF),
        ),
        in_specs=[anywhere] * 4,
        out_specs=(inside, inside, anywhere, anywhere),
        scratch_shapes=[
            vmem((2, 2, NP, 4, 2, TB, DB), BF),
            vmem((NCH, 2, DB, CH), BF),
            vmem((NCH, 2, CH, DB), BF),
            vmem((NIT, 2, 4, ZB, CH), BF),
            vmem((NIT, 2, 2, ZB // 2, CH), BF),
            vmem((NIT, 2, 2, ZB, CH), BF),
            vmem((NCH, 2, NP, 4, ZB, CH), BF),
            vmem((AS, 2, 2, TP, DB), F32),
            vmem((AS, 2, 2, 4, 2, TB, DB), BF),
            vmem((NP, 2, 2, 2, TB, DB), BF),
            vmem((NP, 2, 2, 2, 2, TB, DB), BF),
            vmem((NP, 2, 2, TH, DB), BF),
            vmem((NP, 2, 2, TB, DB), BF),
            vmem((2, DB, CH), BF),
            vmem((2, CH, DB), BF),
            vmem((NCH, DB, CH), BF),
            vmem((NCH, CH, DB), BF),
            vmem((DB, CH), F32),
            vmem((CH, DB), F32),
            dma((NP, 2)),
            dma((NCH, 2)),
            dma((NCH, 2, 2)),
            dma((NCH, 2, 2)),
            dma((NP, 4, 2, 2)),
            dma((NP, 4, 2, 2)),
            dma((NIT, 2, 2)),
            dma((NIT, 2, 2)),
            dma((NIT, 2, 2)),
            dma((NIT, 2, 2)),
            dma((NP, 4, 2, 2)),
            dma((NP, 4, 2, 2)),
            dma((2, 2)),
            dma((NCH, 2)),
            dma((NCH, 2)),
            dma((NCH, 2)),
        ],
        compiler_params=pltpu.CompilerParams(
            collective_id=0, has_side_effects=True, vmem_limit_bytes=62 * 2**20
        ),
        cost_estimate=pl.CostEstimate(flops=29 * 10**9, bytes_accessed=20 * 10**6, transcendentals=10**6),
        name="block",
    )(tokens, cotangent, up_weight, down_weight)
    return mlp, ig, ug.astype(F32), dg.astype(F32)


def solution(mesh):
    fine = Mesh(mesh.devices.reshape(4, 2, 4, 2, 2), AXES)
    rows = P(("dp", "x", "yl"), ("z", "yh"))
    return jax.shard_map(
        on_device,
        mesh=fine,
        in_specs=(rows, P(("z", "yh"), ("x", "yl")), P(("x", "yl"), ("z", "yh")), rows),
        out_specs=(rows, rows, P(("z", "yh"), ("x", "yl", "dp")), P(("x", "yl", "dp"), ("z", "yh"))),
        check_vma=False,
    )
```

time: 288 us -> 226 us (0.78)
  Pallas kernels: 279 us -> 215 us
    pallas_call x1, Pallas kernels: 279 us -> 215 us  [on_device(): pl.pallas_call(kernel, out_shape=(jax.ShapeDtypeStruct((NP * TB, DB), BF)...]
where the time goes in v3:
time: 226 us; the launch traced here: 224 us
  Pallas kernels  215 us (95%)
  other arithmetic  7.19 us (3%)
    pallas_call x1, Pallas kernels, on_device(): pl.pallas_call(kernel, out_shape=(jax.ShapeDtypeStruct((NP * TB, DB), BF)...  215 us
    convert_element_type x2, other arithmetic, on_device(): return (mlp, ig, ug.astype(F32), dg.astype(F32))  7.19 us

profile of v3, /device:TPU:0, one launch (start us, length us, event | category | flops | bytes accessed | tf_op | source)
XLA Modules:
  0.0 223.8 jit_solution(698442415653163142)
XLA Ops:
  0.6 214.6 %block.1 = (bf16[128,768]{1,0:T(8,128)(2,1)}, bf16[128,768]{1,0:T(8,128)(2,1)}, bf16[768,1536]{1,0:T(8,128)(2,1)}, bf16[1536,768]{1,0:T(8,128)(2,1)}) custom-call(bf16[128,768]{1,0:T(8,128)(2,1)} %tok.1, bf16[128,768]{1,0:T(8,128)(2,1)} %cot.1, bf16[768,3072]{1,0:T(8,128)(2,1)} %w1.1, bf16[3072,768]{1,0:T(8,128)(2,1)} %w2.1), custom_call_target="tpu_custom_call" | custom-call | flops 28999999488 | bytes 20000000 | tf_op jit(solution)/shard_map/block/pallas_call | solution.py:453
  215.3 0.0 copy-start
  215.3 4.6 %convert_element_type.6 = f32[768,1536]{1,0:T(8,128)} convert(bf16[768,1536]{1,0:T(8,128)(2,1)} %get-tuple-element.10) | non-fusion elementwise | flops 1179648 | bytes 7077888 | tf_op jit(solution)/shard_map/convert_element_type | solution.py:506
  219.9 0.0 copy-done
  219.9 0.0 copy-start.2
  219.9 0.0 copy-start.1
  219.9 2.5 %convert_element_type.7 = f32[1536,768]{1,0:T(8,128)} convert(bf16[1536,768]{1,0:T(8,128)(2,1)S(1)} %copy-done) | non-fusion elementwise | flops 1179648 | bytes 7077888 | tf_op jit(solution)/shard_map/convert_element_type | solution.py:506
  222.5 0.0 copy-done.2
  222.5 0.7 copy.10
  223.2 0.0 copy-done.1
  223.2 0.7 copy.11
Async XLA Ops:
  215.3 4.7 %copy-start = (bf16[1536,768]{1,0:T(8,128)(2,1)S(1)}, bf16[1536,768]{1,0:T(8,128)(2,1)}, u32[]{:S(2)}) copy-start(bf16[1536,768]{1,0:T(8,128)(2,1)} %get-tuple-element.11) | copy-start | bytes 7077892
  219.9 2.6 %copy-start.2 = (bf16[128,768]{1,0:T(8,128)(2,1)S(1)}, bf16[128,768]{1,0:T(8,128)(2,1)}, u32[]{:S(2)}) copy-start(bf16[128,768]{1,0:T(8,128)(2,1)} %get-tuple-element.16) | copy-start | bytes 589828
  219.9 3.2 %copy-start.1 = (bf16[128,768]{1,0:T(8,128)(2,1)S(1)}, bf16[128,768]{1,0:T(8,128)(2,1)}, u32[]{:S(2)}) copy-start(bf16[128,768]{1,0:T(8,128)(2,1)} %get-tuple-element.17) | copy-start | bytes 589828

commit v4 on v3

--- a/solution.py
+++ b/solution.py
@@ -28,21 +28,21 @@
     "ag0", "ag1", "ag2", "ag3", "ag_wait", "rs0", "rs1", "rs2", "rs3", "rs4", "dw", "fin", "nop",
 )
 STEPS = (
-    320, 321, 160, 352, 353, 323, 192, 384, 355, 224, 322, 197, 385, 256, 165, 416,
-    417, 354, 261, 288, 387, 161, 229, 386, 325, 448, 0, 193, 293, 5, 32, 419,
-    324, 162, 37, 225, 418, 64, 257, 356, 69, 357, 194, 289, 449, 96, 11, 1,
-    7, 164, 101, 6, 326, 43, 388, 33, 39, 38, 258, 327, 196, 226, 389, 75,
-    65, 290, 8, 2, 228, 359, 70, 195, 71, 97, 421, 260, 34, 40, 420, 163,
-    103, 102, 292, 10, 4, 66, 391, 259, 358, 128, 450, 107, 72, 227, 42, 134,
-    98, 390, 36, 291, 3, 104, 9, 74, 423, 129, 35, 422, 68, 130, 41, 12,
-    67, 133, 13, 100, 451, 19, 18, 99, 20, 44, 14, 132, 50, 131, 481, 106,
-    73, 76, 480, 82, 51, 513, 135, 138, 105, 45, 139, 136, 108, 512, 114, 15,
-    83, 137, 46, 77, 483, 140, 482, 146, 52, 640, 545, 115, 17, 544, 78, 109,
-    21, 47, 84, 577, 147, 576, 672, 49, 515, 141, 641, 110, 16, 53, 116, 514,
-    79, 81, 608, 142, 609, 547, 673, 48, 148, 85, 642, 111, 22, 546, 80, 117,
-    23, 54, 113, 579, 674, 143, 112, 149, 55, 643, 86, 145, 144, 485, 87, 118,
-    484, 578, 675, 119, 517, 150, 644, 611, 151, 516, 610, 487, 549, 676, 645, 486,
-    519, 548, 677, 518, 551, 550, 580, 581, 583, 582, 613, 615, 612, 614,
+    320, 321, 323, 195, 352, 322, 353, 355, 163, 326, 384, 327, 385, 354, 192, 259,
+    227, 160, 416, 417, 256, 358, 291, 387, 359, 196, 224, 448, 3, 386, 164, 288,
+    0, 35, 260, 32, 419, 193, 325, 67, 324, 418, 228, 161, 64, 391, 390, 99,
+    292, 4, 449, 6, 96, 10, 36, 9, 165, 38, 128, 42, 357, 356, 68, 257,
+    225, 423, 41, 70, 197, 422, 74, 289, 7, 1, 229, 162, 73, 131, 100, 451,
+    389, 39, 33, 261, 194, 388, 18, 102, 293, 5, 11, 71, 226, 23, 65, 22,
+    258, 103, 37, 420, 421, 132, 290, 43, 8, 106, 97, 21, 134, 69, 75, 135,
+    2, 450, 14, 40, 129, 13, 107, 138, 105, 72, 20, 12, 34, 139, 50, 104,
+    16, 137, 101, 17, 66, 136, 482, 44, 483, 82, 19, 98, 133, 76, 514, 15,
+    51, 130, 45, 108, 480, 481, 114, 47, 83, 515, 546, 55, 77, 140, 146, 640,
+    52, 46, 513, 115, 578, 53, 109, 54, 547, 672, 512, 84, 147, 78, 141, 641,
+    87, 579, 85, 116, 545, 110, 86, 544, 673, 48, 610, 119, 148, 142, 117, 79,
+    642, 611, 118, 577, 576, 149, 151, 150, 111, 487, 674, 486, 49, 143, 643, 80,
+    519, 518, 81, 609, 112, 675, 608, 113, 144, 644, 145, 484, 551, 485, 550, 676,
+    516, 517, 645, 582, 583, 548, 549, 677, 614, 580, 581, 612, 615, 613,
 )
 
 

time: 226 us -> 209 us (0.925)
  Pallas kernels: 215 us -> 198 us
    pallas_call x1, Pallas kernels: 215 us -> 198 us  [on_device(): pl.pallas_call(kernel, out_shape=(jax.ShapeDtypeStruct((NP * TB, DB), BF)...]
where the time goes in v4:
time: 209 us; the launch traced here: 207 us
  Pallas kernels  198 us (95%)
  other arithmetic  7.19 us (3%)
    pallas_call x1, Pallas kernels, on_device(): pl.pallas_call(kernel, out_shape=(jax.ShapeDtypeStruct((NP * TB, DB), BF)...  198 us
    convert_element_type x2, other arithmetic, on_device(): return (mlp, ig, ug.astype(F32), dg.astype(F32))  7.19 us

profile of v4, /device:TPU:0, one launch (start us, length us, event | category | flops | bytes accessed | tf_op | source)
XLA Modules:
  0.0 207.1 jit_solution(12665531714194818843)
XLA Ops:
  0.6 197.9 %block.1 = (bf16[128,768]{1,0:T(8,128)(2,1)}, bf16[128,768]{1,0:T(8,128)(2,1)}, bf16[768,1536]{1,0:T(8,128)(2,1)}, bf16[1536,768]{1,0:T(8,128)(2,1)}) custom-call(bf16[128,768]{1,0:T(8,128)(2,1)} %tok.1, bf16[128,768]{1,0:T(8,128)(2,1)} %cot.1, bf16[768,3072]{1,0:T(8,128)(2,1)} %w1.1, bf16[3072,768]{1,0:T(8,128)(2,1)} %w2.1), custom_call_target="tpu_custom_call" | custom-call | flops 28999999488 | bytes 20000000 | tf_op jit(solution)/shard_map/block/pallas_call | solution.py:453
  198.5 0.0 copy-start
  198.6 4.6 %convert_element_type.6 = f32[768,1536]{1,0:T(8,128)} convert(bf16[768,1536]{1,0:T(8,128)(2,1)} %get-tuple-element.10) | non-fusion elementwise | flops 1179648 | bytes 7077888 | tf_op jit(solution)/shard_map/convert_element_type | solution.py:506
  203.2 0.0 copy-done
  203.2 0.0 copy-start.2
  203.2 0.0 copy-start.1
  203.2 2.5 %convert_element_type.7 = f32[1536,768]{1,0:T(8,128)} convert(bf16[1536,768]{1,0:T(8,128)(2,1)S(1)} %copy-done) | non-fusion elementwise | flops 1179648 | bytes 7077888 | tf_op jit(solution)/shard_map/convert_element_type | solution.py:506
  205.8 0.0 copy-done.2
  205.8 0.7 copy.10
  206.4 0.0 copy-done.1
  206.4 0.7 copy.11
Async XLA Ops:
  198.5 4.7 %copy-start = (bf16[1536,768]{1,0:T(8,128)(2,1)S(1)}, bf16[1536,768]{1,0:T(8,128)(2,1)}, u32[]{:S(2)}) copy-start(bf16[1536,768]{1,0:T(8,128)(2,1)} %get-tuple-element.11) | copy-start | bytes 7077892
  203.2 2.6 %copy-start.2 = (bf16[128,768]{1,0:T(8,128)(2,1)S(1)}, bf16[128,768]{1,0:T(8,128)(2,1)}, u32[]{:S(2)}) copy-start(bf16[128,768]{1,0:T(8,128)(2,1)} %get-tuple-element.16) | copy-start | bytes 589828
  203.2 3.2 %copy-start.1 = (bf16[128,768]{1,0:T(8,128)(2,1)S(1)}, bf16[128,768]{1,0:T(8,128)(2,1)}, u32[]{:S(2)}) copy-start(bf16[128,768]{1,0:T(8,128)(2,1)} %get-tuple-element.17) | copy-start | bytes 589828

commit v5 on v4

--- a/solution.py
+++ b/solution.py
@@ -23,6 +23,7 @@
 NIT = NP * NCH
 ZB = TP // 4
 TH = TB // 2
+WB = 4
 OPS = (
     "start", "merge", "gelu", "spread", "use", "w_far0", "w_far1", "w_sib0", "w_sib1", "w_wait",
     "ag0", "ag1", "ag2", "ag3", "ag_wait", "rs0", "rs1", "rs2", "rs3", "rs4", "dw", "fin", "nop",
@@ -443,6 +444,13 @@
         return carry
 
     lax.fori_loop(0, NIT, drain, 0)
+
+
+def widen(mlp, ig, ug, dg, mlp_out, ig_out, ug_out, dg_out):
+    mlp_out[...] = mlp[...]
+    ig_out[...] = ig[...]
+    ug_out[...] = ug[...].astype(F32)
+    dg_out[...] = dg[...].astype(F32)
 
 
 def on_device(tokens, up_weight, down_weight, cotangent):
@@ -503,7 +511,21 @@
         cost_estimate=pl.CostEstimate(flops=29 * 10**9, bytes_accessed=20 * 10**6, transcendentals=10**6),
         name="block",
     )(tokens, cotangent, up_weight, down_weight)
-    return mlp, ig, ug.astype(F32), dg.astype(F32)
+    return pl.pallas_call(
+        widen,
+        grid=(WB,),
+        out_shape=(
+            jax.ShapeDtypeStruct(mlp.shape, BF),
+            jax.ShapeDtypeStruct(ig.shape, BF),
+            jax.ShapeDtypeStruct(ug.shape, F32),
+            jax.ShapeDtypeStruct(dg.shape, F32),
+        ),
+        in_specs=[pl.BlockSpec((a.shape[0] // WB, a.shape[1]), lambda n: (n, 0)) for a in (mlp, ig, ug, dg)],
+        out_specs=tuple(
+            pl.BlockSpec((a.shape[0] // WB, a.shape[1]), lambda n: (n, 0)) for a in (mlp, ig, ug, dg)
+        ),
+        name="widen",
+    )(mlp, ig, ug, dg)
 
 
 def solution(mesh):

time: 209 us -> 207 us (level)
  other arithmetic: 7.19 us -> 0 us
  Pallas kernels: 198 us -> 205 us
    convert_element_type x2 -> x0, other arithmetic: 7.19 us -> none  [on_device(): return (mlp, ig, ug.astype(F32), dg.astype(F32))]
    pallas_call x0 -> x1, Pallas kernels: none -> 6.69 us  [on_device(): pl.pallas_call(widen, grid=(WB,), out_shape=(jax.ShapeDtypeStruct(mlp.sha...]
where the time goes in v5:
time: 207 us; the launch traced here: 205 us
  Pallas kernels  205 us (99%)
    pallas_call x1, Pallas kernels, on_device(): pl.pallas_call(kernel, out_shape=(jax.ShapeDtypeStruct((NP * TB, DB), BF)...  198 us
    pallas_call x1, Pallas kernels, on_device(): pl.pallas_call(widen, grid=(WB,), out_shape=(jax.ShapeDtypeStruct(mlp.sha...  6.69 us

profile of v5, /device:TPU:0, one launch (start us, length us, event | category | flops | bytes accessed | tf_op | source)
XLA Modules:
  0.0 205.2 jit_solution(14615500574288177776)
XLA Ops:
  0.6 197.9 %block.1 = (bf16[128,768]{1,0:T(8,128)(2,1)}, bf16[128,768]{1,0:T(8,128)(2,1)}, bf16[768,1536]{1,0:T(8,128)(2,1)}, bf16[1536,768]{1,0:T(8,128)(2,1)}) custom-call(bf16[128,768]{1,0:T(8,128)(2,1)} %tok.1, bf16[128,768]{1,0:T(8,128)(2,1)} %cot.1, bf16[768,3072]{1,0:T(8,128)(2,1)} %w1.1, bf16[3072,768]{1,0:T(8,128)(2,1)} %w2.1), custom_call_target="tpu_custom_call" | custom-call | flops 28999999488 | bytes 20000000 | tf_op jit(solution)/shard_map/block/pallas_call | solution.py:461
  198.5 6.7 %widen.1 = (bf16[128,768]{1,0:T(8,128)(2,1)}, bf16[128,768]{1,0:T(8,128)(2,1)}, f32[768,1536]{1,0:T(8,128)}, f32[1536,768]{1,0:T(8,128)}) custom-call(bf16[128,768]{1,0:T(8,128)(2,1)} %get-tuple-element.8.mlp, bf16[128,768]{1,0:T(8,128)(2,1)} %get-tuple-element.9.ig, bf16[768,1536]{1,0:T(8,128)(2,1)} %get-tuple-element.10.ug, ...), custom_call_target="tpu_custom_call" | custom-call | tf_op jit(solution)/shard_map/widen/pallas_call | solution.py:514
